TPU v7x, 32 devices: a whole 2x2x4 slice. The times are simulated.
32 devices in a mesh: groups: 2 (over y), slab: 4 (over z), chan: 4 (over x, core).
Axes of the slice: x: 2, y: 2, z: 4, core: 2. Of those that a mesh axis runs over, the one named last changes fastest.
Arguments:
- field: bfloat16 [40, 64, 4, 128, 128], P(('groups', 'chan'), 'slab'), parts along dimension 0, may hold values from -6 to 6
- spec_weight: bfloat16 [20, 20, 1024, 128], P('chan', None, 'slab'), may hold values from -6 to 6
- mix_weight: bfloat16 [20, 20], replicated, may hold values from -1.25 to 1.25
- bias: float32 [20], P('chan'), may hold values from -4 to 4
- cotangent: bfloat16 [40, 64, 4, 128, 128], P(('groups', 'chan'), 'slab'), parts along dimension 0, may hold values from -6 to 6
Outputs:
- output: bfloat16 [40, 64, 4, 128, 128], P(('groups', 'chan'), 'slab'), parts along dimension 0
- grad_field: bfloat16 [40, 64, 4, 128, 128], P(('groups', 'chan'), 'slab'), parts along dimension 0
- grad_weight: bfloat16 [40, 20, 1024, 128], P(('groups', 'chan'), None, 'slab'), parts along dimension 0
There are 2 independent parts, one for each index of `groups`. A program takes and returns all parts, laid end to end along the dimension named above; an argument that names none is the same for every part. Nothing has to cross between parts.
All inputs are finite; a program needn't handle non-finite values.
Results may differ from a plain program's by a relative error of at most 0.023.
Values may be sent and summed in bfloat16 or wider, within the bound.
A program may use at most 256 MiB of HBM per device.

v0:
```python
import math

import jax
import jax.numpy as jnp
from jax import lax
from jax.sharding import PartitionSpec as P

NX = 128
NY = 128
NZ = 64
NT = 4
KX = 32
KY = 32
KZ = 32


def fourier_rows(count, length):
    rows = jnp.arange(count)
    points = jnp.arange(length)
    freq = (rows + 1) // 2
    phase = freq[:, None] * points[None, :] % length
    angle = phase.astype(jnp.float32) * (2.0 * math.pi / length)
    use_cos = (rows % 2 == 1) | (rows == 0)
    table = jnp.where(use_cos[:, None], jnp.cos(angle), jnp.sin(angle))
    return table * math.sqrt(2.0 / length)


def make_tables():
    table_x = fourier_rows(KX, NX).astype(jnp.bfloat16)
    table_y = fourier_rows(KY, NY).astype(jnp.bfloat16)
    depth = fourier_rows(KZ, NZ)
    times = fourier_rows(NT, NT)
    table_zt = (depth[:, None, :, None] * times[None, :, None, :]).reshape(KZ * NT, NZ * NT)
    return (table_x, table_y, table_zt.astype(jnp.bfloat16))


def analyse(values, table_x, table_y, table_zt):
    first = jnp.einsum(
        "cztxy,ky->cztxk", values, table_y, preferred_element_type=jnp.float32
    ).astype(jnp.bfloat16)
    second = jnp.einsum(
        "cztxk,jx->cztjk", first, table_x, preferred_element_type=jnp.float32
    ).astype(jnp.bfloat16)
    second = second.reshape(second.shape[0], second.shape[1] * NT, KX * KY)
    owned = lax.all_to_all(second, "slab", split_axis=2, concat_axis=1, tiled=True)
    return jnp.einsum("mz,czk->ckm", table_zt, owned, preferred_element_type=jnp.float32).astype(
        jnp.bfloat16
    )


def synthesise(coeffs, table_x, table_y, table_zt):
    slabs = jnp.einsum("mz,okm->ozk", table_zt, coeffs, preferred_element_type=jnp.float32).astype(
        jnp.bfloat16
    )
    local = lax.all_to_all(slabs, "slab", split_axis=1, concat_axis=2, tiled=True)
    depth_cells = local.shape[1] // NT
    local = local.reshape(local.shape[0], depth_cells, NT, KX, KY)
    first = jnp.einsum(
        "oztjk,jx->oztxk", local, table_x, preferred_element_type=jnp.float32
    ).astype(jnp.bfloat16)
    return jnp.einsum("oztxk,ky->oztxy", first, table_y, preferred_element_type=jnp.float32)


def fold_mix(values, matrix):
    return jnp.einsum(
        "oc,cztxy->oztxy",
        matrix,
        lax.all_gather(values, "chan", axis=0, tiled=True),
        preferred_element_type=jnp.float32,
    )


def body(field, spec_weight, mix_weight, bias, cotangent):
    table_x, table_y, table_zt = make_tables()
    local_ch = field.shape[0]
    coeffs = analyse(field, table_x, table_y, table_zt)
    partial_value = jnp.einsum(
        "cokm,ckm->okm", spec_weight, coeffs, preferred_element_type=jnp.float32
    )
    mixed = lax.psum_scatter(
        partial_value.astype(jnp.bfloat16), "chan", scatter_dimension=0, tiled=True
    )
    spectral = synthesise(mixed, table_x, table_y, table_zt)
    transposed_weight = mix_weight.T
    offset = lax.axis_index("chan") * local_ch
    own_rows = lax.dynamic_slice_in_dim(mix_weight, offset, local_ch, 0)
    own_columns = lax.dynamic_slice_in_dim(transposed_weight, offset, local_ch, 0)
    pointwise = fold_mix(field, own_rows)
    pre = spectral + pointwise + bias[:, None, None, None, None]
    activated, pullback = jax.vjp(jax.nn.gelu, pre)
    output = activated.astype(jnp.bfloat16)
    grad_pre = pullback(cotangent.astype(jnp.float32))[0].astype(jnp.bfloat16)
    grad_coeffs = analyse(grad_pre, table_x, table_y, table_zt)
    all_grad = lax.all_gather(grad_coeffs, "chan", axis=0, tiled=True)
    grad_weight = (coeffs.astype(jnp.float32)[:, None] * all_grad.astype(jnp.float32)[None]).astype(
        jnp.bfloat16
    )
    back_coeffs = jnp.einsum(
        "cokm,okm->ckm", spec_weight, all_grad, preferred_element_type=jnp.float32
    ).astype(jnp.bfloat16)
    back = synthesise(back_coeffs, table_x, table_y, table_zt)
    transposed = fold_mix(grad_pre, own_columns)
    grad_field = (back + transposed).astype(jnp.bfloat16)
    return (output, grad_field, grad_weight)


def solution(mesh):
    return jax.shard_map(
        body,
        mesh=mesh,
        in_specs=(
            P(("groups", "chan"), "slab", None, None, None),
            P("chan", None, "slab", None),
            P(),
            P("chan"),
            P(("groups", "chan"), "slab", None, None, None),
        ),
        out_specs=(
            P(("groups", "chan"), "slab", None, None, None),
            P(("groups", "chan"), "slab", None, None, None),
            P(("groups", "chan"), None, "slab", None),
        ),
        check_vma=False,
    )
```

profile of v0, /device:TPU:0, one launch (start us, length us, event | category | flops | bytes accessed | tf_op | source)
XLA Modules:
  0.0 814.4 jit_solution(18182264521689361638)
XLA Ops:
  7.2 11.9 %convert_bitcast_fusion.1 = bf16[5,16,4,32,32]{4,3,2,1,0:T(8,128)(2,1)S(1)} fusion(bf16[5,16,4,128,128]{4,3,2,1,0:T(8,128)(2,1)} %param.5, s32[32]{0:T(128)S(1)} %and_select_fusion.2, pred[32]{0:T(512)(128)(4,1)S(1)} %compare_or_fusion.1), kind=kOutput, calls=%fused_computation.36 | convolution fusion | flops 421208064 | bytes 11141280 | tf_op jit(solution)/shard_map/cztxk,jx->cztjk/dot_general | solution.py:41
  19.1 2.9 reshape.203
  25.9 6.3 all-to-all-start
  33.1 4.2 reshape.208
  37.3 12.2 %all-to-all-done = bf16[4,2,40960]{2,1,0:T(2,128)(2,1)S(1)} async-done(((bf16[4,2,40960]{2,1,0:T(2,128)(2,1)}), bf16[4,2,40960]{2,1,0:T(2,128)(2,1)S(1)}, u32[]{:S(2)}, u32[]{:S(2)}) %all-to-all-start) | async-done | bytes 655392 | tf_op jit(solution)/shard_map/all_to_all | solution.py:45
  52.7 5.7 multiply_reduce_fusion.1
  59.1 25.1 %reduce-scatter.2.cloned.1.call-done = bf16[5,256,128]{2,1,0:T(8,128)(2,1)} async-done(((bf16[20,256,128]{2,1,0:T(8,128)(2,1)}), bf16[5,256,128]{2,1,0:T(8,128)(2,1)}) %reduce-scatter.2.cloned.1.call-update) | async-done | bytes 327696 | tf_op jit(solution)/shard_map/reduce_scatter | solution.py:80
  87.2 4.6 all-to-all-start.1
  91.8 25.7 %all-to-all-done.1 = bf16[5,256,256]{2,0,1:T(8,128)(2,1)S(1)} async-done(((bf16[5,256,256]{2,0,1:T(8,128)(2,1)}), bf16[5,256,256]{2,0,1:T(8,128)(2,1)S(1)}, u32[]{:S(2)}, u32[]{:S(2)}) %all-to-all-start.1) | async-done | bytes 655392 | tf_op jit(solution)/shard_map/all_to_all | solution.py:55
  118.9 3.2 reshape.204
  122.1 214.2 %all-gather.4.cloned.1.call-done = bf16[20,16,4,128,128]{4,3,2,1,0:T(8,128)(2,1)} async-done(((bf16[5,16,4,128,128]{4,3,2,1,0:T(8,128)(2,1)}), bf16[20,16,4,128,128]{4,3,2,1,0:T(8,128)(2,1)}) %all-gather.4.cloned.1.call-update) | async-done | bytes 41943056 | tf_op jit(solution)/shard_map/all_gather | solution.py:68
  336.3 48.3 %fusion.2 = f32[5,16,4,128,128]{4,0,3,2,1:T(8,128)} fusion(bf16[20,16,4,128,128]{4,3,2,1,0:T(8,128)(2,1)} %all-gather.4.cloned.1.call-done, bf16[20,20]{1,0:T(8,128)(2,1)S(1)} %copy-done, s32[]{:T(128)S(6)} %select_n.216), kind=kOutput, calls=%fused_computation.2 | convolution fusion | flops 209715200 | bytes 62916612 | tf_op jit(solution)/shard_map/oc,cztxy->oztxy/dot_general | solution.py:65
  384.5 36.1 %fusion.6 = (bf16[5,16,4,128,128]{4,3,2,1,0:T(8,128)(2,1)}, bf16[5,16,4,128,128]{4,3,2,1,0:T(8,128)(2,1)}) fusion(bf16[5,16,4,128,128]{4,3,2,1,0:T(8,128)(2,1)} %param.9, f32[5]{0:T(128)S(1)} %copy-done.1, f32[5,16,4,128,128]{4,0,3,2,1:T(8,128)} %fusion.2, s32[32]{0:T(128)S(1)} %and_select_fusion.2, pred[32]{0:T(512)(128)(4,1)S(1)} %compare_or_fusion.1, ...), kind=kOutput, calls=%fused_computation.10 | convolution fusion | flops 551952384 | bytes 53084340 | tf_op jit(solution)/shard_map/oztxk,ky->oztxy/dot_general | solution.py:61
  420.7 11.8 %convert_bitcast_fusion = bf16[5,16,4,32,32]{4,3,2,1,0:T(8,128)(2,1)S(1)} fusion(bf16[5,16,4,128,128]{4,3,2,1,0:T(8,128)(2,1)} %get-tuple-element.3, s32[32]{0:T(128)S(1)} %and_select_fusion.2, pred[32]{0:T(512)(128)(4,1)S(1)} %compare_or_fusion.1), kind=kOutput, calls=%fused_computation.32 | convolution fusion | flops 421208064 | bytes 11141280 | tf_op jit(solution)/shard_map/cztxk,jx->cztjk/dot_general | solution.py:41
  432.5 4.0 reshape.205
  441.4 22.4 %all_to_all.66 = bf16[4,2,40960]{2,1,0:T(2,128)(2,1)} all-to-all(bf16[4,2,40960]{2,1,0:T(2,128)(2,1)} %reshape.218), channel_id=1, replica_groups=mesh['groups'=2,'slab'=4,'chan'=4] {'slab'}, dimensions={0} | all-to-all | bytes 1310720 | tf_op jit(solution)/shard_map/all_to_all | solution.py:45
  471.5 15.9 %all-gather.6.cloned.1.call-done = bf16[20,256,128]{2,1,0:T(8,128)(2,1)} async-done(((bf16[5,256,128]{2,1,0:T(8,128)(2,1)}), bf16[20,256,128]{2,1,0:T(8,128)(2,1)}) %all-gather.6.cloned.1.call-update) | async-done | bytes 1310736 | tf_op jit(solution)/shard_map/all_gather | solution.py:94
  489.6 4.2 multiply_reduce_fusion
  497.6 4.6 all-to-all-start.3
  502.2 5.9 multiply_convert_fusion.1
  508.0 20.4 %all-to-all-done.3 = bf16[5,256,256]{2,0,1:T(8,128)(2,1)} async-done(((bf16[5,256,256]{2,0,1:T(8,128)(2,1)}), bf16[5,256,256]{2,0,1:T(8,128)(2,1)}, u32[]{:S(2)}, u32[]{:S(2)}) %all-to-all-start.3) | async-done | bytes 655392 | tf_op jit(solution)/shard_map/all_to_all | solution.py:55
  531.3 208.7 %all-gather.8.cloned.1.call-done = bf16[20,16,4,128,128]{4,3,2,1,0:T(8,128)(2,1)} async-done(((bf16[5,16,4,128,128]{4,3,2,1,0:T(8,128)(2,1)}), bf16[20,16,4,128,128]{4,3,2,1,0:T(8,128)(2,1)}) %all-gather.8.cloned.1.call-update) | async-done | bytes 41943056 | tf_op jit(solution)/shard_map/all_gather | solution.py:68
  740.0 49.5 %fusion = f32[5,16,4,128,128]{4,0,3,2,1:T(8,128)} fusion(bf16[20,16,4,128,128]{4,3,2,1,0:T(8,128)(2,1)} %all-gather.8.cloned.1.call-done, bf16[20,20]{1,0:T(8,128)(2,1)S(1)} %copy-done, s32[]{:T(128)S(6)} %select_n.216), kind=kOutput, calls=%fused_computation | convolution fusion | flops 209715200 | bytes 62915364 | tf_op jit(solution)/shard_map/oc,cztxy->oztxy/dot_general | solution.py:65
  789.5 18.1 %fusion.14 = bf16[5,16,4,128,128]{4,3,2,1,0:T(8,128)(2,1)} fusion(f32[5,16,4,128,128]{4,0,3,2,1:T(8,128)} %fusion, bf16[5,16,4,32,32]{4,3,2,1,0:T(8,128)(2,1)S(1)} %reshape.206, s32[32]{0:T(128)S(1)} %and_select_fusion.2, pred[32]{0:T(512)(128)(4,1)S(1)} %compare_or_fusion.1), kind=kOutput, calls=%fused_computation.19 | convolution fusion | flops 431366144 | bytes 32112800 | tf_op jit(solution)/shard_map/oztxk,ky->oztxy/dot_general | solution.py:61
  (39 shorter events, 34.5 us)
Async XLA Ops:
  7.2 329.1 %copy-start = (bf16[20,20]{1,0:T(8,128)(2,1)S(1)}, bf16[20,20]{1,0:T(8,128)(2,1)}, u32[]{:S(2)}) copy-start(bf16[20,20]{1,0:T(8,128)(2,1)} %param.7) | copy-start | bytes 2404
  25.9 23.6 %all-to-all-start = ((bf16[4,2,40960]{2,1,0:T(2,128)(2,1)}), bf16[4,2,40960]{2,1,0:T(2,128)(2,1)S(1)}, u32[]{:S(2)}, u32[]{:S(2)}) async-start(bf16[4,2,40960]{2,1,0:T(2,128)(2,1)} %reshape.216), calls=%async_computation | async-start | bytes 1310720 | tf_op jit(solution)/shard_map/all_to_all | solution.py:45
  32.2 52.0 %reduce-scatter.2.cloned.1.call-start = ((), (), s32[]{:S(2)}) async-start(), calls=%async_computation.5 | async-start | bytes 1638400 | tf_op jit(solution)/shard_map/reduce_scatter | solution.py:80
  58.4 277.9 %all-gather.4.cloned.1.call-start = ((), (), s32[]{:S(2)}) async-start(), calls=%async_computation.6 | async-start | bytes 52428800 | tf_op jit(solution)/shard_map/all_gather | solution.py:68
  87.2 30.3 %all-to-all-start.1 = ((bf16[5,256,256]{2,0,1:T(8,128)(2,1)}), bf16[5,256,256]{2,0,1:T(8,128)(2,1)S(1)}, u32[]{:S(2)}, u32[]{:S(2)}) async-start(bf16[5,256,256]{2,0,1:T(8,128)(2,1)} %copy.45), calls=%async_computation.2 | async-start | bytes 2097152 | tf_op jit(solution)/shard_map/all_to_all | solution.py:55
  91.8 395.7 %all-gather.6.cloned.1.call-start = ((), (), s32[]{:S(2)}) async-start(), calls=%async_computation.7 | async-start | bytes 1638400 | tf_op jit(solution)/shard_map/all_gather | solution.py:94
  122.1 262.5 %copy-start.1 = (f32[5]{0:T(128)S(1)}, f32[5]{0:T(128)}, u32[]{:S(2)}) copy-start(f32[5]{0:T(128)} %param.8) | copy-start | bytes 64
  471.0 269.0 %all-gather.8.cloned.1.call-start = ((), (), s32[]{:S(2)}) async-start(), calls=%async_computation.8 | async-start | bytes 52428800 | tf_op jit(solution)/shard_map/all_gather | solution.py:68
  497.6 30.8 %all-to-all-start.3 = ((bf16[5,256,256]{2,0,1:T(8,128)(2,1)}), bf16[5,256,256]{2,0,1:T(8,128)(2,1)}, u32[]{:S(2)}, u32[]{:S(2)}) async-start(bf16[5,256,256]{2,0,1:T(8,128)(2,1)} %copy.55), calls=%async_computation.4 | async-start | bytes 2097152 | tf_op jit(solution)/shard_map/all_to_all | solution.py:55
Sparse Core Ops, SparseCore 0:
  58.5 25.6 reduce-scatter.1
  85.8 250.3 all-gather.3
  471.1 16.3 all-gather.5
  489.5 250.4 all-gather.7
where the time goes:
time: 824 us; the launch traced here: 814 us
  waiting for transfers between devices  523 us (63%)
  matrix products  180 us (22%)
  local copies, waits for them, and re-layouts  40.5 us (5%)
  blocking collectives  22.4 us (3%)
  other arithmetic  18.7 us (2%)
  starting transfers between devices  15.8 us (2%)
  between operations  14.1 us (2%)
    all_gather x2, waiting for transfers between devices, fold_mix(): lax.all_gather(values, 'chan', axis=0, tiled=True)  423 us
    dot_general x2, matrix products, fold_mix(): jnp.einsum('oc,cztxy->oztxy', matrix, lax.all_gather(values, 'chan', axis...  97.8 us
    dot_general x2, matrix products, synthesise(): jnp.einsum('oztxk,ky->oztxy', first, table_y, preferred_element_type=jnp....  54.3 us
    all_to_all x2, waiting for transfers between devices, synthesise(): lax.all_to_all(slabs, 'slab', split_axis=1, concat_axis=2, tiled=True)  46.1 us
    reduce_scatter x1, waiting for transfers between devices, body(): lax.psum_scatter(partial_value.astype(jnp.bfloat16), 'chan', scatter_dime...  25.1 us
    dot_general x2, matrix products, analyse(): jnp.einsum('cztxk,jx->cztjk', first, table_x, preferred_element_type=jnp....  23.7 us
    all_to_all x1, blocking collectives, analyse(): lax.all_to_all(second, 'slab', split_axis=2, concat_axis=1, tiled=True)  22.4 us
  transfers between devices with their start and end apart: 7, of which 7 were waited for; matrix products, arithmetic and copies ran while one was open for 4% of the time, Pallas kernels for 0%

commit v1 on v0

v1 whole, which is shorter than its diff:
```python
import math

import jax
import jax.numpy as jnp
from jax import lax
from jax.experimental import pallas as pl
from jax.experimental.pallas import tpu as pltpu
from jax.sharding import PartitionSpec as P

NX = 128
NY = 128
NZ = 64
NT = 4
KX = 32
KY = 32
KZ = 32
CHUNKS = 4
TILE = 16
VMEM_BYTES = 40 * 1024 * 1024


def fourier_rows(count, length):
    rows = jnp.arange(count)
    points = jnp.arange(length)
    freq = (rows + 1) // 2
    phase = freq[:, None] * points[None, :] % length
    angle = phase.astype(jnp.float32) * (2.0 * math.pi / length)
    use_cos = (rows % 2 == 1) | (rows == 0)
    table = jnp.where(use_cos[:, None], jnp.cos(angle), jnp.sin(angle))
    return table * math.sqrt(2.0 / length)


def make_tables():
    table_x = fourier_rows(KX, NX).astype(jnp.bfloat16)
    table_y = fourier_rows(KY, NY).astype(jnp.bfloat16)
    depth = fourier_rows(KZ, NZ)
    times = fourier_rows(NT, NT)
    table_zt = (depth[:, None, :, None] * times[None, :, None, :]).reshape(KZ * NT, NZ * NT)
    return (table_x, table_y, table_zt.astype(jnp.bfloat16))


def analyse_xy(values, table_x, table_y):
    first = jnp.einsum(
        "cnxy,ky->cnxk", values, table_y, preferred_element_type=jnp.float32
    ).astype(jnp.bfloat16)
    second = jnp.einsum(
        "cnxk,jx->cnjk", first, table_x, preferred_element_type=jnp.float32
    ).astype(jnp.bfloat16)
    return second.reshape(second.shape[0], second.shape[1], KX * KY)


def analyse_zt(second, table_zt):
    owned = lax.all_to_all(second, "slab", split_axis=2, concat_axis=1, tiled=True)
    return jnp.einsum("mz,czk->ckm", table_zt, owned, preferred_element_type=jnp.float32).astype(
        jnp.bfloat16
    )


def synthesise_zt(coeffs, table_zt):
    slabs = jnp.einsum("mz,okm->ozk", table_zt, coeffs, preferred_element_type=jnp.float32).astype(
        jnp.bfloat16
    )
    local = lax.all_to_all(slabs, "slab", split_axis=1, concat_axis=2, tiled=True)
    count, cells = local.shape[:2]
    local = local.reshape(count, cells, KX, KY).transpose(1, 2, 0, 3)
    return local.reshape(cells, KX, count * KY)


def mix_pair(own_ref, other_ref, weights, row, pair):
    halves = []
    for half in range(2):
        lines = pl.ds((2 * pair + half) * TILE, TILE)
        mine = own_ref[:, row, lines, :]
        theirs = other_ref[:, row, lines, :]
        shape = (mine.shape[0] * TILE, mine.shape[2])
        halves.append(jnp.concatenate([mine.reshape(shape), theirs.reshape(shape)], axis=0))
    return jnp.dot(
        weights, jnp.concatenate(halves, axis=1), preferred_element_type=jnp.float32
    )


def spectral_rows(spec_ref, tx_ref, ty_ref, row):
    first = jnp.dot(tx_ref[...], spec_ref[row], preferred_element_type=jnp.float32)
    return jnp.dot(
        first.astype(jnp.bfloat16), ty_ref[...], preferred_element_type=jnp.float32
    )


def partial_kernel(weight_ref, own_ref, other_ref, out_ref):
    weights = weight_ref[...]
    count, rows, nx, ny = out_ref.shape
    for row in range(rows):
        for pair in range(nx // (2 * TILE)):
            mixed = mix_pair(own_ref, other_ref, weights, row, pair).astype(jnp.bfloat16)
            for half in range(2):
                part = mixed[:, half * ny : (half + 1) * ny]
                out_ref[:, row, pl.ds((2 * pair + half) * TILE, TILE), :] = part.reshape(
                    count, TILE, ny
                )


def forward_kernel(*refs):
    weight_ref, tx_ref, ty_ref, bias_ref, own_ref, other_ref, part_ref, spec_ref, cot_ref = refs[:9]
    out_ref, grad_ref, pre_ref = refs[-3:]
    weights = weight_ref[...]
    count, rows, nx, ny = out_ref.shape
    scale = math.sqrt(2.0 / math.pi)
    cubic = 0.044715
    for row in range(rows):
        pre_ref[...] = spectral_rows(spec_ref, tx_ref, ty_ref, row)
        for pair in range(nx // (2 * TILE)):
            mixed = mix_pair(own_ref, other_ref, weights, row, pair)
            for half in range(2):
                lines = pl.ds((2 * pair + half) * TILE, TILE)
                for o in range(count):
                    pre = (
                        mixed[o * TILE : (o + 1) * TILE, half * ny : (half + 1) * ny]
                        + pre_ref[lines, o * ny : (o + 1) * ny]
                        + part_ref[o, row, lines, :].astype(jnp.float32)
                        + bias_ref[o]
                    )
                    square = pre * pre
                    bent = jnp.tanh(scale * (pre + cubic * (pre * square)))
                    half_up = 0.5 * (1.0 + bent)
                    slope = half_up + (0.5 * pre) * (1.0 - bent * bent) * (
                        scale * (1.0 + (3.0 * cubic) * square)
                    )
                    out_ref[o, row, lines, :] = (pre * half_up).astype(jnp.bfloat16)
                    cot = cot_ref[o, row, lines, :].astype(jnp.float32)
                    grad_ref[o, row, lines, :] = (cot * slope).astype(jnp.bfloat16)


def backward_kernel(*refs):
    weight_ref, tx_ref, ty_ref, own_ref, other_ref, part_ref, spec_ref = refs[:7]
    out_ref, pre_ref = refs[-2:]
    weights = weight_ref[...]
    count, rows, nx, ny = out_ref.shape
    for row in range(rows):
        pre_ref[...] = spectral_rows(spec_ref, tx_ref, ty_ref, row)
        for pair in range(nx // (2 * TILE)):
            mixed = mix_pair(own_ref, other_ref, weights, row, pair)
            for half in range(2):
                lines = pl.ds((2 * pair + half) * TILE, TILE)
                for o in range(count):
                    total = (
                        mixed[o * TILE : (o + 1) * TILE, half * ny : (half + 1) * ny]
                        + pre_ref[lines, o * ny : (o + 1) * ny]
                        + part_ref[o, row, lines, :].astype(jnp.float32)
                    )
                    out_ref[o, row, lines, :] = total.astype(jnp.bfloat16)


class Local:
    def __init__(self, shape):
        self.shape = shape
        self.count, self.cells, self.nx, self.ny = shape
        self.size = self.cells // CHUNKS
        self.block = math.gcd(self.size, 2)
        self.steps = self.size // self.block

    def rows(self, chunk=None):
        base = 0 if chunk is None else chunk * self.steps
        return pl.BlockSpec(
            (self.count, self.block, self.nx, self.ny), lambda i: (0, base + i, 0, 0)
        )

    def whole(self, array):
        return pl.BlockSpec(array.shape, lambda i: (0,) * array.ndim)

    def spectra(self, chunk):
        base = chunk * self.steps
        return pl.BlockSpec((self.block, KX, self.count * KY), lambda i: (base + i, 0, 0))

    def piece(self):
        return jax.ShapeDtypeStruct((self.count, self.size, self.nx, self.ny), jnp.bfloat16)

    def cost(self, arrays, dots):
        cells = self.count * self.size * self.nx * self.ny
        return pl.CostEstimate(
            flops=dots * cells * 2 * self.count * TILE, bytes_accessed=arrays * 2 * cells,
            transcendentals=0,
        )

    def params(self):
        return pltpu.CompilerParams(
            dimension_semantics=("arbitrary",), vmem_limit_bytes=VMEM_BYTES
        )

    def scratch(self):
        return [pltpu.VMEM((self.nx, self.count * self.ny), jnp.float32)]

    def partial(self, weights, own, other, chunk):
        return pl.pallas_call(
            partial_kernel,
            grid=(self.steps,),
            in_specs=[self.whole(weights), self.rows(chunk), self.rows()],
            out_specs=self.rows(),
            out_shape=self.piece(),
            compiler_params=self.params(),
            cost_estimate=self.cost(3, 2),
        )(weights, own, other)

    def forward(self, weights, tables, bias, own, other, part, spec, cot, chunk, held):
        args = [weights, *tables, bias, own, other, part, spec, cot]
        specs = [self.whole(weights), *[self.whole(t) for t in tables]]
        specs += [pl.BlockSpec(memory_space=pltpu.SMEM)]
        specs += [self.rows(chunk), self.rows(), self.rows(), self.spectra(chunk), self.rows(chunk)]
        aliases = {}
        if held is not None:
            aliases = {len(args): 0}
            args.append(held)
            specs.append(pl.BlockSpec(memory_space=pl.ANY))
        return pl.pallas_call(
            forward_kernel,
            grid=(self.steps,),
            in_specs=specs,
            out_specs=[self.rows(chunk), self.rows()],
            out_shape=[jax.ShapeDtypeStruct(self.shape, jnp.bfloat16), self.piece()],
            scratch_shapes=self.scratch(),
            input_output_aliases=aliases,
            compiler_params=self.params(),
            cost_estimate=self.cost(7, 4),
        )(*args)

    def backward(self, weights, tables, own, other, part, spec, chunk, held):
        args = [weights, *tables, own, other, part, spec]
        specs = [self.whole(weights), *[self.whole(t) for t in tables]]
        specs += [self.rows(), self.rows(), self.rows(), self.spectra(chunk)]
        aliases = {}
        if held is not None:
            aliases = {len(args): 0}
            args.append(held)
            specs.append(pl.BlockSpec(memory_space=pl.ANY))
        return pl.pallas_call(
            backward_kernel,
            grid=(self.steps,),
            in_specs=specs,
            out_specs=self.rows(chunk),
            out_shape=jax.ShapeDtypeStruct(self.shape, jnp.bfloat16),
            scratch_shapes=self.scratch(),
            input_output_aliases=aliases,
            compiler_params=self.params(),
            cost_estimate=self.cost(4, 3),
        )(*args)


def spread(matrix):
    eye = jnp.eye(TILE, dtype=matrix.dtype)
    rows, columns = matrix.shape
    return (matrix[:, None, :, None] * eye[None, :, None, :]).reshape(rows * TILE, columns * TILE)


def body(field, spec_weight, mix_weight, bias, cotangent):
    table_x, table_y, table_zt = make_tables()
    full_shape = field.shape
    count = full_shape[0]
    shape = (count, full_shape[1] * full_shape[2], full_shape[3], full_shape[4])
    field = field.reshape(shape)
    cotangent = cotangent.reshape(shape)
    local = Local(shape)
    parts = mix_weight.shape[0] // count
    across = [(i, i ^ 2) for i in range(parts)]
    beside = [(i, i ^ 1) for i in range(parts)]
    me = lax.axis_index("chan")

    eye = jnp.eye(count, dtype=table_y.dtype)
    wide_y = (eye[:, None, :, None] * table_y[None, :, None, :]).reshape(
        count * KY, count * shape[3]
    )
    tables = (table_x.T, wide_y)

    def weights_for(matrix):
        def block(row, column):
            return lax.dynamic_slice(matrix, (row * count, column * count), (count, count))

        return [
            spread(jnp.concatenate([block(row, me), block(row, me ^ 2)], axis=1))
            for row in (me, me ^ 1)
        ]

    own_weights, beside_weights = weights_for(mix_weight)
    own_back, beside_back = weights_for(mix_weight.T)

    def cut(values, chunk):
        return values[:, chunk * local.size : (chunk + 1) * local.size]

    others = [lax.ppermute(cut(field, k), "chan", across) for k in range(CHUNKS)]
    coeffs = analyse_zt(analyse_xy(field, table_x, table_y), table_zt)
    partial_value = jnp.einsum(
        "cokm,ckm->okm", spec_weight, coeffs, preferred_element_type=jnp.float32
    )
    mixed = lax.psum_scatter(
        partial_value.astype(jnp.bfloat16), "chan", scatter_dimension=0, tiled=True
    )
    spectra = synthesise_zt(mixed, table_zt)
    shares = [
        lax.ppermute(local.partial(beside_weights, field, others[k], k), "chan", beside)
        for k in range(CHUNKS)
    ]
    output, grads, seconds, grad_others = None, [], [], []
    for k in range(CHUNKS):
        output, grad = local.forward(
            own_weights, tables, bias, field, others[k], shares[k], spectra, cotangent, k, output
        )
        grads.append(grad)
        grad_others.append(lax.ppermute(grad, "chan", across))
        seconds.append(analyse_xy(grad, table_x, table_y))
    grad_coeffs = analyse_zt(jnp.concatenate(seconds, axis=1), table_zt)
    all_grad = lax.all_gather(grad_coeffs, "chan", axis=0, tiled=True)
    grad_weight = (coeffs.astype(jnp.float32)[:, None] * all_grad.astype(jnp.float32)[None]).astype(
        jnp.bfloat16
    )
    back_coeffs = jnp.einsum(
        "cokm,okm->ckm", spec_weight, all_grad, preferred_element_type=jnp.float32
    ).astype(jnp.bfloat16)
    back = synthesise_zt(back_coeffs, table_zt)
    grad_shares = [
        lax.ppermute(
            local_partial(local, beside_back, grads[k], grad_others[k]), "chan", beside
        )
        for k in range(CHUNKS)
    ]
    grad_field = None
    for k in range(CHUNKS):
        grad_field = local.backward(
            own_back, tables, grads[k], grad_others[k], grad_shares[k], back, k, grad_field
        )
    return (output.reshape(full_shape), grad_field.reshape(full_shape), grad_weight)


def local_partial(local, weights, own, other):
    return local.partial(weights, own, other, 0)


def solution(mesh):
    return jax.shard_map(
        body,
        mesh=mesh,
        in_specs=(
            P(("groups", "chan"), "slab", None, None, None),
            P("chan", None, "slab", None),
            P(),
            P("chan"),
            P(("groups", "chan"), "slab", None, None, None),
        ),
        out_specs=(
            P(("groups", "chan"), "slab", None, None, None),
            P(("groups", "chan"), "slab", None, None, None),
            P(("groups", "chan"), None, "slab", None),
        ),
        check_vma=False,
    )
```

time: 824 us -> 742 us (0.900)
  matrix products: 180 us -> 31.3 us
  Pallas kernels: 0 us -> 135 us
  waiting for transfers between devices: 523 us -> 427 us
  local copies, waits for them, and re-layouts: 40.5 us -> 72.5 us
  blocking collectives: 22.4 us -> 0 us
  starting transfers between devices: 15.8 us -> 29 us
    all_gather x2 -> x0, waiting for transfers between devices: 423 us -> none  [fold_mix(): lax.all_gather(values, 'chan', axis=0, tiled=True)]
    ppermute x0 -> x16, waiting for transfers between devices: none -> 369 us  [the longest x4 186 us: body(): lax.ppermute(cut(field, k), 'chan', across)]
    dot_general x10, matrix products: 180 us -> 31.3 us  [the longest x5 18.8 us: analyse_xy(): jnp.einsum('cnxk,jx->cnjk', first, table_x, preferred_element_type=jnp.fl...]
    pallas_call x0 -> x16, Pallas kernels: none -> 135 us  [the longest x8 55.4 us: partial(): pl.pallas_call(partial_kernel, grid=(self.steps,), in_specs=[self.whole(w...]
    reduce_scatter x1, waiting for transfers between devices: 25.1 us -> 0.02 us  [body(): lax.psum_scatter(partial_value.astype(jnp.bfloat16), 'chan', scatter_dime...]
    all_to_all x1 -> x0, blocking collectives: 22.4 us -> none  [analyse(): lax.all_to_all(second, 'slab', split_axis=2, concat_axis=1, tiled=True)]
    all_gather x1, waiting for transfers between devices: 15.9 us -> 0.01 us  [body(): all_grad = lax.all_gather(grad_coeffs, 'chan', axis=0, tiled=True)]
    unnamed x8 -> x59, local copies, waits for them, and re-layouts: 8.76 us -> 23.2 us
  transfers between devices with their start and end apart: 7 -> 22, of which waited for: 7 -> 11; matrix products, arithmetic and copies ran while one was open for 4% -> 10% of each run, Pallas kernels for 0% -> 16%
where the time goes in v1:
time: 742 us; the launch traced here: 734 us
  waiting for transfers between devices  427 us (58%)
  Pallas kernels  135 us (18%)
  local copies, waits for them, and re-layouts  72.5 us (10%)
  matrix products  31.3 us (4%)
  starting transfers between devices  29 us (4%)
  other arithmetic  24.1 us (3%)
  between operations  14.8 us (2%)
    ppermute x4, waiting for transfers between devices, body(): lax.ppermute(cut(field, k), 'chan', across)  186 us
    ppermute x4, waiting for transfers between devices, body(): grad_others.append(lax.ppermute(grad, 'chan', across))  183 us
    pallas_call x8, Pallas kernels, partial(): pl.pallas_call(partial_kernel, grid=(self.steps,), in_specs=[self.whole(w...  55.4 us
    all_to_all x2, waiting for transfers between devices, synthesise_zt(): lax.all_to_all(slabs, 'slab', split_axis=1, concat_axis=2, tiled=True)  45.3 us
    pallas_call x4, Pallas kernels, forward(): pl.pallas_call(forward_kernel, grid=(self.steps,), in_specs=specs, out_sp...  45.2 us
    pallas_call x4, Pallas kernels, backward(): pl.pallas_call(backward_kernel, grid=(self.steps,), in_specs=specs, out_s...  34.7 us
    unnamed x59, local copies, waits for them, and re-layouts  23.2 us
    dot_general x5, matrix products, analyse_xy(): jnp.einsum('cnxk,jx->cnjk', first, table_x, preferred_element_type=jnp.fl...  18.8 us
  transfers between devices with their start and end apart: 22, of which 11 were waited for; matrix products, arithmetic and copies ran while one was open for 10% of the time, Pallas kernels for 16%

profile of v1, /device:TPU:0, one launch (start us, length us, event | category | flops | bytes accessed | tf_op | source)
XLA Modules:
  0.0 734.2 jit_solution(12118116409606486437)
XLA Ops:
  7.2 7.8 %convert_bitcast_fusion = bf16[5,64,128,32]{2,3,1,0:T(8,128)(2,1)S(1)} fusion(bf16[5,64,128,128]{3,2,1,0:T(8,128)(2,1)} %bitcast.122, s32[32]{0:T(128)S(1)} %and_select_fusion.2, pred[32]{0:T(512)(128)(4,1)S(1)} %compare_or_fusion.1), kind=kOutput, calls=%fused_computation.6 | convolution fusion | flops 336924672 | bytes 13107360 | tf_op jit(solution)/shard_map/cnxy,ky->cnxk/dot_general | solution.py:43
  28.2 9.1 %fusion.99 = (bf16[5,16,128,128]{3,2,1,0:T(8,128)(2,1)}, bf16[5,16,128,128]{3,2,1,0:T(8,128)(2,1)}, bf16[5,16,128,128]{3,2,1,0:T(8,128)(2,1)}, bf16[5,16,128,128]{3,2,1,0:T(8,128)(2,1)}) fusion(bf16[5,64,128,128]{3,2,1,0:T(8,128)(2,1)} %bitcast.123), kind=kLoop, calls=%fused_computation.137 | loop fusion | bytes 20971520 | tf_op jit(solution)/shard_map/slice | solution.py:285
  64.3 40.1 %collective-permute-done.6.other_ref.refs_5_ = bf16[5,16,128,128]{3,2,1,0:T(8,128)(2,1)} collective-permute-done((bf16[5,16,128,128]{3,2,1,0:T(8,128)(2,1)}, bf16[5,16,128,128]{3,2,1,0:T(8,128)(2,1)}, u32[]{:S(2)}, u32[]{:S(2)}) %collective-permute-start.6) | collective-permute-done | bytes 2621472 | tf_op jit(solution)/shard_map/ppermute | solution.py:287
  104.4 7.2 shard_map.79
  111.6 49.0 %collective-permute-done.4.other_ref.refs_5_ = bf16[5,16,128,128]{3,2,1,0:T(8,128)(2,1)} collective-permute-done((bf16[5,16,128,128]{3,2,1,0:T(8,128)(2,1)}, bf16[5,16,128,128]{3,2,1,0:T(8,128)(2,1)}, u32[]{:S(2)}, u32[]{:S(2)}) %collective-permute-start.4) | collective-permute-done | bytes 2621472 | tf_op jit(solution)/shard_map/ppermute | solution.py:287
  160.6 7.2 shard_map.78
  167.8 49.0 %collective-permute-done.2.other_ref.refs_5_ = bf16[5,16,128,128]{3,2,1,0:T(8,128)(2,1)} collective-permute-done((bf16[5,16,128,128]{3,2,1,0:T(8,128)(2,1)}, bf16[5,16,128,128]{3,2,1,0:T(8,128)(2,1)}, u32[]{:S(2)}, u32[]{:S(2)}) %collective-permute-start.2) | collective-permute-done | bytes 2621472 | tf_op jit(solution)/shard_map/ppermute | solution.py:287
  216.8 7.2 shard_map.77
  224.0 47.4 %collective-permute-done.other_ref.refs_5_ = bf16[5,16,128,128]{3,2,1,0:T(8,128)(2,1)S(1)} collective-permute-done((bf16[5,16,128,128]{3,2,1,0:T(8,128)(2,1)}, bf16[5,16,128,128]{3,2,1,0:T(8,128)(2,1)S(1)}, u32[]{:S(2)}, u32[]{:S(2)}) %collective-permute-start) | collective-permute-done | bytes 2621472 | tf_op jit(solution)/shard_map/ppermute | solution.py:287
  287.3 25.5 %all-to-all-done.1 = bf16[5,256,256]{2,0,1:T(8,128)(2,1)S(1)} async-done(((bf16[5,256,256]{2,0,1:T(8,128)(2,1)}), bf16[5,256,256]{2,0,1:T(8,128)(2,1)S(1)}, u32[]{:S(2)}, u32[]{:S(2)}) %all-to-all-start.1) | async-done | bytes 655392 | tf_op jit(solution)/shard_map/all_to_all | solution.py:63
  317.6 11.3 %shard_map.80 = (bf16[5,64,128,128]{3,2,1,0:T(8,128)(2,1)}, bf16[5,16,128,128]{3,2,1,0:T(8,128)(2,1)S(1)}) custom-call(bf16[80,160]{1,0:T(8,128)(2,1)S(1)} %mul.646.refs_0_, bf16[128,32]{1,0:T(8,128)(2,1)S(1)} %multiply_convert_fusion.2.refs_1_, bf16[160,640]{1,0:T(8,128)(2,1)S(1)} %bitcast.114, f32[5]{0:T(128)S(1)} %copy-done.15, ...), custom_call_target="tpu_custom_call" | custom-call | flops 838860800 | bytes 18350080 | tf_op jit(solution)/shard_map/pallas_call | solution.py:213
  330.5 11.3 %shard_map.81 = (bf16[5,64,128,128]{3,2,1,0:T(8,128)(2,1)}, bf16[5,16,128,128]{3,2,1,0:T(8,128)(2,1)S(1)}) custom-call(bf16[80,160]{1,0:T(8,128)(2,1)S(1)} %mul.646.refs_0_, bf16[128,32]{1,0:T(8,128)(2,1)S(1)} %multiply_convert_fusion.2.refs_1_, bf16[160,640]{1,0:T(8,128)(2,1)S(1)} %bitcast.115, f32[5]{0:T(128)S(1)} %copy-done.15, ...), custom_call_target="tpu_custom_call", output_to_operand_aliasing={{0}: (9, {})} | custom-call | flops 838860800 | bytes 18350080 | tf_op jit(solution)/shard_map/pallas_call | solution.py:213
  343.4 11.5 %shard_map.82 = (bf16[5,64,128,128]{3,2,1,0:T(8,128)(2,1)}, bf16[5,16,128,128]{3,2,1,0:T(8,128)(2,1)S(1)}) custom-call(bf16[80,160]{1,0:T(8,128)(2,1)S(1)} %mul.646.refs_0_, bf16[128,32]{1,0:T(8,128)(2,1)S(1)} %multiply_convert_fusion.2.refs_1_, bf16[160,640]{1,0:T(8,128)(2,1)S(1)} %bitcast.116, f32[5]{0:T(128)S(1)} %copy-done.15, ...), custom_call_target="tpu_custom_call", output_to_operand_aliasing={{0}: (9, {})} | custom-call | flops 838860800 | bytes 18350080 | tf_op jit(solution)/shard_map/pallas_call | solution.py:213
  356.4 11.1 %shard_map.83 = (bf16[5,64,128,128]{3,2,1,0:T(8,128)(2,1)}, bf16[5,16,128,128]{3,2,1,0:T(8,128)(2,1)S(1)}) custom-call(bf16[80,160]{1,0:T(8,128)(2,1)S(1)} %mul.646.refs_0_, bf16[128,32]{1,0:T(8,128)(2,1)S(1)} %multiply_convert_fusion.2.refs_1_, bf16[160,640]{1,0:T(8,128)(2,1)S(1)} %bitcast.117, f32[5]{0:T(128)S(1)} %copy-done.15, ...), custom_call_target="tpu_custom_call", output_to_operand_aliasing={{0}: (9, {})} | custom-call | flops 838860800 | bytes 18350080 | tf_op jit(solution)/shard_map/pallas_call | solution.py:213
  407.8 13.0 %all-to-all-done.2 = bf16[4,2,40960]{2,1,0:T(2,128)(2,1)} async-done(((bf16[4,2,40960]{2,1,0:T(2,128)(2,1)}), bf16[4,2,40960]{2,1,0:T(2,128)(2,1)}, u32[]{:S(2)}, u32[]{:S(2)}) %all-to-all-start.2) | async-done | bytes 655392 | tf_op jit(solution)/shard_map/all_to_all | solution.py:53
  432.6 38.3 %collective-permute-done.14.other_ref.refs_4_ = bf16[5,16,128,128]{3,2,1,0:T(8,128)(2,1)} collective-permute-done((bf16[5,16,128,128]{3,2,1,0:T(8,128)(2,1)}, bf16[5,16,128,128]{3,2,1,0:T(8,128)(2,1)}, u32[]{:S(2)}, u32[]{:S(2)}) %collective-permute-start.14) | collective-permute-done | bytes 2621472 | tf_op jit(solution)/shard_map/ppermute | solution.py:306
  479.3 47.8 %collective-permute-done.12.other_ref.refs_4_ = bf16[5,16,128,128]{3,2,1,0:T(8,128)(2,1)} collective-permute-done((bf16[5,16,128,128]{3,2,1,0:T(8,128)(2,1)}, bf16[5,16,128,128]{3,2,1,0:T(8,128)(2,1)}, u32[]{:S(2)}, u32[]{:S(2)}) %collective-permute-start.12) | collective-permute-done | bytes 2621472 | tf_op jit(solution)/shard_map/ppermute | solution.py:306
  533.8 49.4 %collective-permute-done.10.other_ref.refs_4_ = bf16[5,16,128,128]{3,2,1,0:T(8,128)(2,1)} collective-permute-done((bf16[5,16,128,128]{3,2,1,0:T(8,128)(2,1)}, bf16[5,16,128,128]{3,2,1,0:T(8,128)(2,1)}, u32[]{:S(2)}, u32[]{:S(2)}) %collective-permute-start.10) | collective-permute-done | bytes 2621472 | tf_op jit(solution)/shard_map/ppermute | solution.py:306
  590.0 47.8 %collective-permute-done.8.other_ref.refs_4_ = bf16[5,16,128,128]{3,2,1,0:T(8,128)(2,1)} collective-permute-done((bf16[5,16,128,128]{3,2,1,0:T(8,128)(2,1)S(1)}, bf16[5,16,128,128]{3,2,1,0:T(8,128)(2,1)}, u32[]{:S(2)}, u32[]{:S(2)}) %collective-permute-start.8) | collective-permute-done | bytes 2621472 | tf_op jit(solution)/shard_map/ppermute | solution.py:306
  665.8 19.8 %all-to-all-done.3 = bf16[5,256,256]{2,0,1:T(8,128)(2,1)S(1)} async-done(((bf16[5,256,256]{2,0,1:T(8,128)(2,1)}), bf16[5,256,256]{2,0,1:T(8,128)(2,1)S(1)}, u32[]{:S(2)}, u32[]{:S(2)}) %all-to-all-start.3) | async-done | bytes 655392 | tf_op jit(solution)/shard_map/all_to_all | solution.py:63
  692.3 8.6 %shard_map.88.refs_7_ = bf16[5,64,128,128]{3,2,1,0:T(8,128)(2,1)} custom-call(bf16[80,160]{1,0:T(8,128)(2,1)S(1)} %mul.682.refs_0_, bf16[128,32]{1,0:T(8,128)(2,1)S(1)} %multiply_convert_fusion.2.refs_1_, bf16[160,640]{1,0:T(8,128)(2,1)S(1)} %bitcast.118, bf16[5,16,128,128]{3,2,1,0:T(8,128)(2,1)S(1)} %copy-done.12, ...), custom_call_target="tpu_custom_call" | custom-call | flops 629145600 | bytes 10485760 | tf_op jit(solution)/shard_map/pallas_call | solution.py:234
  700.9 8.7 %shard_map.89.refs_7_ = bf16[5,64,128,128]{3,2,1,0:T(8,128)(2,1)} custom-call(bf16[80,160]{1,0:T(8,128)(2,1)S(1)} %mul.682.refs_0_, bf16[128,32]{1,0:T(8,128)(2,1)S(1)} %multiply_convert_fusion.2.refs_1_, bf16[160,640]{1,0:T(8,128)(2,1)S(1)} %bitcast.119, bf16[5,16,128,128]{3,2,1,0:T(8,128)(2,1)S(1)} %copy-done.6, ...), custom_call_target="tpu_custom_call", output_to_operand_aliasing={{}: (7, {})} | custom-call | flops 629145600 | bytes 10485760 | tf_op jit(solution)/shard_map/pallas_call | solution.py:234
  709.6 8.8 %shard_map.90.refs_7_ = bf16[5,64,128,128]{3,2,1,0:T(8,128)(2,1)} custom-call(bf16[80,160]{1,0:T(8,128)(2,1)S(1)} %mul.682.refs_0_, bf16[128,32]{1,0:T(8,128)(2,1)S(1)} %multiply_convert_fusion.2.refs_1_, bf16[160,640]{1,0:T(8,128)(2,1)S(1)} %bitcast.120, bf16[5,16,128,128]{3,2,1,0:T(8,128)(2,1)S(1)} %copy-done.9, ...), custom_call_target="tpu_custom_call", output_to_operand_aliasing={{}: (7, {})} | custom-call | flops 629145600 | bytes 10485760 | tf_op jit(solution)/shard_map/pallas_call | solution.py:234
  718.4 8.6 %shard_map.91 = bf16[5,64,128,128]{3,2,1,0:T(8,128)(2,1)} custom-call(bf16[80,160]{1,0:T(8,128)(2,1)S(1)} %mul.682.refs_0_, bf16[128,32]{1,0:T(8,128)(2,1)S(1)} %multiply_convert_fusion.2.refs_1_, bf16[160,640]{1,0:T(8,128)(2,1)S(1)} %bitcast.121, bf16[5,16,128,128]{3,2,1,0:T(8,128)(2,1)S(1)} %copy-done.2, ...), custom_call_target="tpu_custom_call", output_to_operand_aliasing={{}: (7, {})} | custom-call | flops 629145600 | bytes 10485760 | tf_op jit(solution)/shard_map/pallas_call | solution.py:234
  (155 shorter events, 173.9 us)
Async XLA Ops:
  21.4 28.0 %all-to-all-start = ((bf16[4,2,40960]{2,1,0:T(2,128)(2,1)}), bf16[4,2,40960]{2,1,0:T(2,128)(2,1)S(1)}, u32[]{:S(2)}, u32[]{:S(2)}) async-start(bf16[4,2,40960]{2,1,0:T(2,128)(2,1)} %reshape.336), calls=%async_computation | async-start | bytes 1310720 | tf_op jit(solution)/shard_map/all_to_all | solution.py:53
  27.7 250.7 %reduce-scatter.2.cloned.1.call-start = ((), (), s32[]{:S(2)}) async-start(), calls=%async_computation.5 | async-start | bytes 1638400 | tf_op jit(solution)/shard_map/reduce_scatter | solution.py:292
  37.3 67.1 %collective-permute-start.6 = (bf16[5,16,128,128]{3,2,1,0:T(8,128)(2,1)}, bf16[5,16,128,128]{3,2,1,0:T(8,128)(2,1)}, u32[]{:S(2)}, u32[]{:S(2)}) collective-permute-start(bf16[5,16,128,128]{3,2,1,0:T(8,128)(2,1)} %get-tuple-element.19), channel_id=1, source_target_pairs={{0,2},{1,3},{2,0},{3,1},{4,6},{5,7},{6,4},{7,5},{8,10},{9,11},{10,... | collective-permute-start | bytes 7864328 | tf_op jit(solution)/shard_map/ppermute | solution.py:287
  38.8 121.8 %collective-permute-start.4 = (bf16[5,16,128,128]{3,2,1,0:T(8,128)(2,1)}, bf16[5,16,128,128]{3,2,1,0:T(8,128)(2,1)}, u32[]{:S(2)}, u32[]{:S(2)}) collective-permute-start(bf16[5,16,128,128]{3,2,1,0:T(8,128)(2,1)} %get-tuple-element.20), channel_id=1, source_target_pairs={{0,2},{1,3},{2,0},{3,1},{4,6},{5,7},{6,4},{7,5},{8,10},{9,11},{10,... | collective-permute-start | bytes 7864328 | tf_op jit(solution)/shard_map/ppermute | solution.py:287
  39.3 177.5 %collective-permute-start.2 = (bf16[5,16,128,128]{3,2,1,0:T(8,128)(2,1)}, bf16[5,16,128,128]{3,2,1,0:T(8,128)(2,1)}, u32[]{:S(2)}, u32[]{:S(2)}) collective-permute-start(bf16[5,16,128,128]{3,2,1,0:T(8,128)(2,1)} %get-tuple-element.21), channel_id=1, source_target_pairs={{0,2},{1,3},{2,0},{3,1},{4,6},{5,7},{6,4},{7,5},{8,10},{9,11},{10,... | collective-permute-start | bytes 7864328 | tf_op jit(solution)/shard_map/ppermute | solution.py:287
  40.8 230.6 %collective-permute-start = (bf16[5,16,128,128]{3,2,1,0:T(8,128)(2,1)}, bf16[5,16,128,128]{3,2,1,0:T(8,128)(2,1)S(1)}, u32[]{:S(2)}, u32[]{:S(2)}) collective-permute-start(bf16[5,16,128,128]{3,2,1,0:T(8,128)(2,1)} %get-tuple-element.22), channel_id=1, source_target_pairs={{0,2},{1,3},{2,0},{3,1},{4,6},{5,7},{6,4},{7,5},{8,10},{9,11},{10,... | collective-permute-start | bytes 7864328 | tf_op jit(solution)/shard_map/ppermute | solution.py:287
  111.6 205.9 %collective-permute-start.7 = (bf16[5,16,128,128]{3,2,1,0:T(8,128)(2,1)}, bf16[5,16,128,128]{3,2,1,0:T(8,128)(2,1)}, u32[]{:S(2)}, u32[]{:S(2)}) collective-permute-start(bf16[5,16,128,128]{3,2,1,0:T(8,128)(2,1)} %shard_map.79), channel_id=1, source_target_pairs={{0,1},{1,0},{2,3},{3,2},{4,5},{5,4},{6,7},{7,6},{8,9},{9,8},{10,11... | collective-permute-start | bytes 7864328 | tf_op jit(solution)/shard_map/ppermute | solution.py:297
  167.8 162.7 %collective-permute-start.5 = (bf16[5,16,128,128]{3,2,1,0:T(8,128)(2,1)}, bf16[5,16,128,128]{3,2,1,0:T(8,128)(2,1)}, u32[]{:S(2)}, u32[]{:S(2)}) collective-permute-start(bf16[5,16,128,128]{3,2,1,0:T(8,128)(2,1)} %shard_map.78), channel_id=1, source_target_pairs={{0,1},{1,0},{2,3},{3,2},{4,5},{5,4},{6,7},{7,6},{8,9},{9,8},{10,11... | collective-permute-start | bytes 7864328 | tf_op jit(solution)/shard_map/ppermute | solution.py:297
  224.0 119.4 %collective-permute-start.3 = (bf16[5,16,128,128]{3,2,1,0:T(8,128)(2,1)}, bf16[5,16,128,128]{3,2,1,0:T(8,128)(2,1)}, u32[]{:S(2)}, u32[]{:S(2)}) collective-permute-start(bf16[5,16,128,128]{3,2,1,0:T(8,128)(2,1)} %shard_map.77), channel_id=1, source_target_pairs={{0,1},{1,0},{2,3},{3,2},{4,5},{5,4},{6,7},{7,6},{8,9},{9,8},{10,11... | collective-permute-start | bytes 7864328 | tf_op jit(solution)/shard_map/ppermute | solution.py:297
  278.3 78.1 %collective-permute-start.1 = (bf16[5,16,128,128]{3,2,1,0:T(8,128)(2,1)}, bf16[5,16,128,128]{3,2,1,0:T(8,128)(2,1)}, u32[]{:S(2)}, u32[]{:S(2)}) collective-permute-start(bf16[5,16,128,128]{3,2,1,0:T(8,128)(2,1)} %shard_map.76), channel_id=1, source_target_pairs={{0,1},{1,0},{2,3},{3,2},{4,5},{5,4},{6,7},{7,6},{8,9},{9,8},{10,11... | collective-permute-start | bytes 7864328 | tf_op jit(solution)/shard_map/ppermute | solution.py:297
  281.4 31.3 %all-to-all-start.1 = ((bf16[5,256,256]{2,0,1:T(8,128)(2,1)}), bf16[5,256,256]{2,0,1:T(8,128)(2,1)S(1)}, u32[]{:S(2)}, u32[]{:S(2)}) async-start(bf16[5,256,256]{2,0,1:T(8,128)(2,1)} %copy.98), calls=%async_computation.2 | async-start | bytes 2097152 | tf_op jit(solution)/shard_map/all_to_all | solution.py:63
  399.4 21.3 %all-to-all-start.2 = ((bf16[4,2,40960]{2,1,0:T(2,128)(2,1)}), bf16[4,2,40960]{2,1,0:T(2,128)(2,1)}, u32[]{:S(2)}, u32[]{:S(2)}) async-start(bf16[4,2,40960]{2,1,0:T(2,128)(2,1)} %reshape.338), calls=%async_computation.3 | async-start | bytes 1310720 | tf_op jit(solution)/shard_map/all_to_all | solution.py:53
  403.6 240.9 %all-gather.2.cloned.1.call-start = ((), (), s32[]{:S(2)}) async-start(), calls=%async_computation.6 | async-start | bytes 1638400 | tf_op jit(solution)/shard_map/all_gather | solution.py:309
  403.7 67.2 %collective-permute-start.14 = (bf16[5,16,128,128]{3,2,1,0:T(8,128)(2,1)}, bf16[5,16,128,128]{3,2,1,0:T(8,128)(2,1)}, u32[]{:S(2)}, u32[]{:S(2)}) collective-permute-start(bf16[5,16,128,128]{3,2,1,0:T(8,128)(2,1)} %copy-done.10), channel_id=1, source_target_pairs={{0,2},{1,3},{2,0},{3,1},{4,6},{5,7},{6,4},{7,5},{8,10},{9,11},{10,... | collective-permute-start | bytes 7864328 | tf_op jit(solution)/shard_map/ppermute | solution.py:306
  405.2 121.8 %collective-permute-start.12 = (bf16[5,16,128,128]{3,2,1,0:T(8,128)(2,1)}, bf16[5,16,128,128]{3,2,1,0:T(8,128)(2,1)}, u32[]{:S(2)}, u32[]{:S(2)}) collective-permute-start(bf16[5,16,128,128]{3,2,1,0:T(8,128)(2,1)} %copy-done.3), channel_id=1, source_target_pairs={{0,2},{1,3},{2,0},{3,1},{4,6},{5,7},{6,4},{7,5},{8,10},{9,11},{10,... | collective-permute-start | bytes 7864328 | tf_op jit(solution)/shard_map/ppermute | solution.py:306
  405.8 177.5 %collective-permute-start.10 = (bf16[5,16,128,128]{3,2,1,0:T(8,128)(2,1)}, bf16[5,16,128,128]{3,2,1,0:T(8,128)(2,1)}, u32[]{:S(2)}, u32[]{:S(2)}) collective-permute-start(bf16[5,16,128,128]{3,2,1,0:T(8,128)(2,1)} %copy-done.7), channel_id=1, source_target_pairs={{0,2},{1,3},{2,0},{3,1},{4,6},{5,7},{6,4},{7,5},{8,10},{9,11},{10,... | collective-permute-start | bytes 7864328 | tf_op jit(solution)/shard_map/ppermute | solution.py:306
  407.3 230.5 %collective-permute-start.8 = (bf16[5,16,128,128]{3,2,1,0:T(8,128)(2,1)S(1)}, bf16[5,16,128,128]{3,2,1,0:T(8,128)(2,1)}, u32[]{:S(2)}, u32[]{:S(2)}) collective-permute-start(bf16[5,16,128,128]{3,2,1,0:T(8,128)(2,1)S(1)} %copy-done.1), channel_id=1, source_target_pairs={{0,2},{1,3},{2,0},{3,1},{4,6},{5,7},{6,4},{7,5},{8,10},{9,11},{10,... | collective-permute-start | bytes 7864328 | tf_op jit(solution)/shard_map/ppermute | solution.py:306
  432.6 94.5 %copy-start.5 = (bf16[5,16,128,128]{3,2,1,0:T(8,128)(2,1)S(1)}, bf16[5,16,128,128]{3,2,1,0:T(8,128)(2,1)}, u32[]{:S(2)}) copy-start(bf16[5,16,128,128]{3,2,1,0:T(8,128)(2,1)} %copy-done.3) | copy-start | bytes 7864324
  479.3 103.9 %copy-start.8 = (bf16[5,16,128,128]{3,2,1,0:T(8,128)(2,1)S(1)}, bf16[5,16,128,128]{3,2,1,0:T(8,128)(2,1)}, u32[]{:S(2)}) copy-start(bf16[5,16,128,128]{3,2,1,0:T(8,128)(2,1)} %copy-done.7) | copy-start | bytes 7864324
  479.3 211.1 %collective-permute-start.15 = (bf16[5,16,128,128]{3,2,1,0:T(8,128)(2,1)}, bf16[5,16,128,128]{3,2,1,0:T(8,128)(2,1)}, u32[]{:S(2)}, u32[]{:S(2)}) collective-permute-start(bf16[5,16,128,128]{3,2,1,0:T(8,128)(2,1)} %shard_map.87), channel_id=1, source_target_pairs={{0,1},{1,0},{2,3},{3,2},{4,5},{5,4},{6,7},{7,6},{8,9},{9,8},{10,11... | collective-permute-start | bytes 7864328 | tf_op jit(solution)/shard_map/ppermute | solution.py:318
  533.8 167.1 %collective-permute-start.13 = (bf16[5,16,128,128]{3,2,1,0:T(8,128)(2,1)}, bf16[5,16,128,128]{3,2,1,0:T(8,128)(2,1)}, u32[]{:S(2)}, u32[]{:S(2)}) collective-permute-start(bf16[5,16,128,128]{3,2,1,0:T(8,128)(2,1)} %shard_map.86), channel_id=1, source_target_pairs={{0,1},{1,0},{2,3},{3,2},{4,5},{5,4},{6,7},{7,6},{8,9},{9,8},{10,11... | collective-permute-start | bytes 7864328 | tf_op jit(solution)/shard_map/ppermute | solution.py:318
  590.0 119.7 %collective-permute-start.11 = (bf16[5,16,128,128]{3,2,1,0:T(8,128)(2,1)}, bf16[5,16,128,128]{3,2,1,0:T(8,128)(2,1)}, u32[]{:S(2)}, u32[]{:S(2)}) collective-permute-start(bf16[5,16,128,128]{3,2,1,0:T(8,128)(2,1)} %shard_map.85), channel_id=1, source_target_pairs={{0,1},{1,0},{2,3},{3,2},{4,5},{5,4},{6,7},{7,6},{8,9},{9,8},{10,11... | collective-permute-start | bytes 7864328 | tf_op jit(solution)/shard_map/ppermute | solution.py:318
  644.5 73.9 %collective-permute-start.9 = (bf16[5,16,128,128]{3,2,1,0:T(8,128)(2,1)}, bf16[5,16,128,128]{3,2,1,0:T(8,128)(2,1)}, u32[]{:S(2)}, u32[]{:S(2)}) collective-permute-start(bf16[5,16,128,128]{3,2,1,0:T(8,128)(2,1)} %shard_map.84), channel_id=1, source_target_pairs={{0,1},{1,0},{2,3},{3,2},{4,5},{5,4},{6,7},{7,6},{8,9},{9,8},{10,11... | collective-permute-start | bytes 7864328 | tf_op jit(solution)/shard_map/ppermute | solution.py:318
  654.6 31.0 %all-to-all-start.3 = ((bf16[5,256,256]{2,0,1:T(8,128)(2,1)}), bf16[5,256,256]{2,0,1:T(8,128)(2,1)S(1)}, u32[]{:S(2)}, u32[]{:S(2)}) async-start(bf16[5,256,256]{2,0,1:T(8,128)(2,1)} %copy.112), calls=%async_computation.4 | async-start | bytes 2097152 | tf_op jit(solution)/shard_map/all_to_all | solution.py:63
  (25 other events, 260.4 us)
Sparse Core Ops, SparseCore 0:
  61.6 35.1 reduce-scatter.1
  431.5 24.4 all-gather.1

commit v2 on v1

--- a/solution.py
+++ b/solution.py
@@ -14,7 +14,6 @@
 KX = 32
 KY = 32
 KZ = 32
-CHUNKS = 4
 TILE = 16
 VMEM_BYTES = 40 * 1024 * 1024
 
@@ -39,31 +38,32 @@
     return (table_x, table_y, table_zt.astype(jnp.bfloat16))
 
 
-def analyse_xy(values, table_x, table_y):
-    first = jnp.einsum(
-        "cnxy,ky->cnxk", values, table_y, preferred_element_type=jnp.float32
-    ).astype(jnp.bfloat16)
-    second = jnp.einsum(
-        "cnxk,jx->cnjk", first, table_x, preferred_element_type=jnp.float32
-    ).astype(jnp.bfloat16)
-    return second.reshape(second.shape[0], second.shape[1], KX * KY)
-
-
-def analyse_zt(second, table_zt):
-    owned = lax.all_to_all(second, "slab", split_axis=2, concat_axis=1, tiled=True)
-    return jnp.einsum("mz,czk->ckm", table_zt, owned, preferred_element_type=jnp.float32).astype(
-        jnp.bfloat16
-    )
+def analyse_zt(second, table_zt, count):
+    if KX % lax.axis_size("slab"):
+        second = second.reshape(second.shape[0], KX, count, KY).transpose(2, 0, 1, 3)
+        second = second.reshape(count, second.shape[1], KX * KY)
+        owned = lax.all_to_all(second, "slab", split_axis=2, concat_axis=1, tiled=True)
+        coeffs = jnp.einsum("mz,czk->ckm", table_zt, owned, preferred_element_type=jnp.float32)
+        return coeffs.astype(jnp.bfloat16)
+    owned = lax.all_to_all(second, "slab", split_axis=1, concat_axis=0, tiled=True)
+    cells, own_x, _ = owned.shape
+    owned = owned.reshape(cells, own_x, count, KY)
+    coeffs = jnp.einsum("mz,zjck->cjkm", table_zt, owned, preferred_element_type=jnp.float32)
+    return coeffs.astype(jnp.bfloat16).reshape(count, own_x * KY, table_zt.shape[0])
 
 
 def synthesise_zt(coeffs, table_zt):
-    slabs = jnp.einsum("mz,okm->ozk", table_zt, coeffs, preferred_element_type=jnp.float32).astype(
-        jnp.bfloat16
-    )
-    local = lax.all_to_all(slabs, "slab", split_axis=1, concat_axis=2, tiled=True)
-    count, cells = local.shape[:2]
-    local = local.reshape(count, cells, KX, KY).transpose(1, 2, 0, 3)
-    return local.reshape(cells, KX, count * KY)
+    count, modes, _ = coeffs.shape
+    if KX % lax.axis_size("slab"):
+        slabs = jnp.einsum("mz,okm->ozk", table_zt, coeffs, preferred_element_type=jnp.float32)
+        slabs = slabs.astype(jnp.bfloat16)
+        local = lax.all_to_all(slabs, "slab", split_axis=1, concat_axis=2, tiled=True)
+        local = local.reshape(count, local.shape[1], KX, KY).transpose(1, 2, 0, 3)
+        return local.reshape(local.shape[0], KX, count * KY)
+    coeffs = coeffs.reshape(count, modes // KY, KY, coeffs.shape[2])
+    slabs = jnp.einsum("mz,ojkm->zjok", table_zt, coeffs, preferred_element_type=jnp.float32)
+    slabs = slabs.astype(jnp.bfloat16).reshape(slabs.shape[0], modes // KY, count * KY)
+    return lax.all_to_all(slabs, "slab", split_axis=0, concat_axis=1, tiled=True)
 
 
 def mix_pair(own_ref, other_ref, weights, row, pair):
@@ -86,7 +86,37 @@
     )
 
 
-def partial_kernel(weight_ref, own_ref, other_ref, out_ref):
+def analyse_row(values_ref, ax_ref, ay_ref, row):
+    count = values_ref.shape[0]
+    values = jnp.concatenate([values_ref[c, row] for c in range(count)], axis=1)
+    first = jnp.dot(ax_ref[...], values, preferred_element_type=jnp.float32)
+    return jnp.dot(
+        first.astype(jnp.bfloat16), ay_ref[...], preferred_element_type=jnp.float32
+    ).astype(jnp.bfloat16)
+
+
+def analysis_kernel(ax_ref, ay_ref, field_ref, second_ref):
+    for row in range(field_ref.shape[1]):
+        second_ref[row] = analyse_row(field_ref, ax_ref, ay_ref, row)
+
+
+def gate_kernel(value_ref, *refs):
+    refs[-1][...] = value_ref[...]
+
+
+def gate(value, *earlier):
+    return pl.pallas_call(
+        gate_kernel,
+        in_specs=[pl.BlockSpec(memory_space=pltpu.VMEM)]
+        + [pl.BlockSpec(memory_space=pl.ANY) for _ in earlier],
+        out_specs=pl.BlockSpec(memory_space=pltpu.VMEM),
+        out_shape=jax.ShapeDtypeStruct(value.shape, value.dtype),
+        compiler_params=pltpu.CompilerParams(vmem_limit_bytes=VMEM_BYTES),
+    )(value, *earlier)
+
+
+def partial_kernel(weight_ref, own_ref, other_ref, token_ref, spec_ref, out_ref, done_ref):
+    done_ref[...] = jnp.zeros_like(done_ref)
     weights = weight_ref[...]
     count, rows, nx, ny = out_ref.shape
     for row in range(rows):
@@ -100,8 +130,10 @@
 
 
 def forward_kernel(*refs):
-    weight_ref, tx_ref, ty_ref, bias_ref, own_ref, other_ref, part_ref, spec_ref, cot_ref = refs[:9]
-    out_ref, grad_ref, pre_ref = refs[-3:]
+    weight_ref, tx_ref, ty_ref, ax_ref, ay_ref, bias_ref = refs[:6]
+    own_ref, other_ref, part_ref, spec_ref, cot_ref = refs[6:11]
+    out_ref, grad_ref, second_ref, done_ref, pre_ref = refs[-5:]
+    done_ref[...] = jnp.zeros_like(done_ref)
     weights = weight_ref[...]
     count, rows, nx, ny = out_ref.shape
     scale = math.sqrt(2.0 / math.pi)
@@ -128,11 +160,13 @@
                     out_ref[o, row, lines, :] = (pre * half_up).astype(jnp.bfloat16)
                     cot = cot_ref[o, row, lines, :].astype(jnp.float32)
                     grad_ref[o, row, lines, :] = (cot * slope).astype(jnp.bfloat16)
+        second_ref[row] = analyse_row(grad_ref, ax_ref, ay_ref, row)
 
 
 def backward_kernel(*refs):
     weight_ref, tx_ref, ty_ref, own_ref, other_ref, part_ref, spec_ref = refs[:7]
-    out_ref, pre_ref = refs[-2:]
+    out_ref, done_ref, pre_ref = refs[-3:]
+    done_ref[...] = jnp.zeros_like(done_ref)
     weights = weight_ref[...]
     count, rows, nx, ny = out_ref.shape
     for row in range(rows):
@@ -151,15 +185,15 @@
 
 
 class Local:
-    def __init__(self, shape):
+    def __init__(self, shape, start, size):
         self.shape = shape
         self.count, self.cells, self.nx, self.ny = shape
-        self.size = self.cells // CHUNKS
-        self.block = math.gcd(self.size, 2)
-        self.steps = self.size // self.block
-
-    def rows(self, chunk=None):
-        base = 0 if chunk is None else chunk * self.steps
+        self.start, self.size = start, size
+        self.block = math.gcd(math.gcd(start, size), 4)
+        self.steps = size // self.block
+
+    def rows(self, inside=False):
+        base = self.start // self.block if inside else 0
         return pl.BlockSpec(
             (self.count, self.block, self.nx, self.ny), lambda i: (0, base + i, 0, 0)
         )
@@ -167,19 +201,15 @@
     def whole(self, array):
         return pl.BlockSpec(array.shape, lambda i: (0,) * array.ndim)
 
-    def spectra(self, chunk):
-        base = chunk * self.steps
+    def spectra(self, inside=False):
+        base = self.start // self.block if inside else 0
         return pl.BlockSpec((self.block, KX, self.count * KY), lambda i: (base + i, 0, 0))
 
     def piece(self):
         return jax.ShapeDtypeStruct((self.count, self.size, self.nx, self.ny), jnp.bfloat16)
 
-    def cost(self, arrays, dots):
-        cells = self.count * self.size * self.nx * self.ny
-        return pl.CostEstimate(
-            flops=dots * cells * 2 * self.count * TILE, bytes_accessed=arrays * 2 * cells,
-            transcendentals=0,
-        )
+    def cost(self):
+        return pl.CostEstimate(flops=1, bytes_accessed=1, transcendentals=0)
 
     def params(self):
         return pltpu.CompilerParams(
@@ -189,22 +219,51 @@
     def scratch(self):
         return [pltpu.VMEM((self.nx, self.count * self.ny), jnp.float32)]
 
-    def partial(self, weights, own, other, chunk):
+    def token(self):
+        return jax.ShapeDtypeStruct((8, 128), jnp.float32)
+
+    def token_spec(self):
+        return pl.BlockSpec((8, 128), lambda i: (0, 0))
+
+    def second(self):
+        return jax.ShapeDtypeStruct((self.size, KX, self.count * KY), jnp.bfloat16)
+
+    def analysis(self, tables, field):
+        return pl.pallas_call(
+            analysis_kernel,
+            grid=(self.steps,),
+            in_specs=[*[self.whole(t) for t in tables], self.rows()],
+            out_specs=self.spectra(),
+            out_shape=self.second(),
+            compiler_params=self.params(),
+            cost_estimate=self.cost(),
+        )(*tables, field)
+
+    def partial(self, weights, own, other, inside, token, spec):
         return pl.pallas_call(
             partial_kernel,
             grid=(self.steps,),
-            in_specs=[self.whole(weights), self.rows(chunk), self.rows()],
-            out_specs=self.rows(),
-            out_shape=self.piece(),
+            in_specs=[
+                self.whole(weights),
+                self.rows(inside),
+                self.rows(inside),
+                self.token_spec(),
+                pl.BlockSpec(memory_space=pl.ANY),
+            ],
+            out_specs=[self.rows(), self.token_spec()],
+            out_shape=[self.piece(), self.token()],
             compiler_params=self.params(),
-            cost_estimate=self.cost(3, 2),
-        )(weights, own, other)
-
-    def forward(self, weights, tables, bias, own, other, part, spec, cot, chunk, held):
-        args = [weights, *tables, bias, own, other, part, spec, cot]
+            cost_estimate=self.cost(),
+        )(weights, own, other, token, spec)
+
+    def forward(
+        self, weights, tables, bias, own, other, part, spec, cot, token, held, earlier
+    ):
+        args = [weights, *tables, bias, own, other, part, spec, cot, token, earlier]
         specs = [self.whole(weights), *[self.whole(t) for t in tables]]
         specs += [pl.BlockSpec(memory_space=pltpu.SMEM)]
-        specs += [self.rows(chunk), self.rows(), self.rows(), self.spectra(chunk), self.rows(chunk)]
+        specs += [self.rows(True), self.rows(True), self.rows(), self.spectra(True), self.rows(True)]
+        specs += [self.token_spec(), pl.BlockSpec(memory_space=pl.ANY)]
         aliases = {}
         if held is not None:
             aliases = {len(args): 0}
@@ -214,18 +273,23 @@
             forward_kernel,
             grid=(self.steps,),
             in_specs=specs,
-            out_specs=[self.rows(chunk), self.rows()],
-            out_shape=[jax.ShapeDtypeStruct(self.shape, jnp.bfloat16), self.piece()],
+            out_specs=[self.rows(True), self.rows(), self.spectra(), self.token_spec()],
+            out_shape=[
+                jax.ShapeDtypeStruct(self.shape, jnp.bfloat16),
+                self.piece(),
+                self.second(),
+                self.token(),
+            ],
             scratch_shapes=self.scratch(),
             input_output_aliases=aliases,
             compiler_params=self.params(),
-            cost_estimate=self.cost(7, 4),
+            cost_estimate=self.cost(),
         )(*args)
 
-    def backward(self, weights, tables, own, other, part, spec, chunk, held):
-        args = [weights, *tables, own, other, part, spec]
+    def backward(self, weights, tables, own, other, part, spec, token, held):
+        args = [weights, *tables, own, other, part, spec, token]
         specs = [self.whole(weights), *[self.whole(t) for t in tables]]
-        specs += [self.rows(), self.rows(), self.rows(), self.spectra(chunk)]
+        specs += [self.rows(), self.rows(), self.rows(), self.spectra(True), self.token_spec()]
         aliases = {}
         if held is not None:
             aliases = {len(args): 0}
@@ -235,12 +299,12 @@
             backward_kernel,
             grid=(self.steps,),
             in_specs=specs,
-            out_specs=self.rows(chunk),
-            out_shape=jax.ShapeDtypeStruct(self.shape, jnp.bfloat16),
+            out_specs=[self.rows(True), self.token_spec()],
+            out_shape=[jax.ShapeDtypeStruct(self.shape, jnp.bfloat16), self.token()],
             scratch_shapes=self.scratch(),
             input_output_aliases=aliases,
             compiler_params=self.params(),
-            cost_estimate=self.cost(4, 3),
+            cost_estimate=self.cost(),
         )(*args)
 
 
@@ -257,7 +321,10 @@
     shape = (count, full_shape[1] * full_shape[2], full_shape[3], full_shape[4])
     field = field.reshape(shape)
     cotangent = cotangent.reshape(shape)
-    local = Local(shape)
+    unit = max(shape[1] // 8, 1)
+    ends = [0, 2 * unit, max(shape[1] - unit, 2 * unit), shape[1]]
+    spans = [Local(shape, a, b - a) for a, b in zip(ends, ends[1:]) if b > a]
+    chunks = len(spans)
     parts = mix_weight.shape[0] // count
     across = [(i, i ^ 2) for i in range(parts)]
     beside = [(i, i ^ 1) for i in range(parts)]
@@ -267,7 +334,8 @@
     wide_y = (eye[:, None, :, None] * table_y[None, :, None, :]).reshape(
         count * KY, count * shape[3]
     )
-    tables = (table_x.T, wide_y)
+    synthesis_tables = (table_x.T, wide_y)
+    analysis_tables = (table_x, wide_y.T)
 
     def weights_for(matrix):
         def block(row, column):
@@ -281,11 +349,10 @@
     own_weights, beside_weights = weights_for(mix_weight)
     own_back, beside_back = weights_for(mix_weight.T)
 
-    def cut(values, chunk):
-        return values[:, chunk * local.size : (chunk + 1) * local.size]
-
-    others = [lax.ppermute(cut(field, k), "chan", across) for k in range(CHUNKS)]
-    coeffs = analyse_zt(analyse_xy(field, table_x, table_y), table_zt)
+    token = jnp.zeros((8, 128), jnp.float32)
+    other = lax.ppermute(field, "chan", across)
+    second = Local(shape, 0, shape[1]).analysis(analysis_tables, field)
+    coeffs = analyse_zt(second, table_zt, count)
     partial_value = jnp.einsum(
         "cokm,ckm->okm", spec_weight, coeffs, preferred_element_type=jnp.float32
     )
@@ -293,20 +360,29 @@
         partial_value.astype(jnp.bfloat16), "chan", scatter_dimension=0, tiled=True
     )
     spectra = synthesise_zt(mixed, table_zt)
-    shares = [
-        lax.ppermute(local.partial(beside_weights, field, others[k], k), "chan", beside)
-        for k in range(CHUNKS)
-    ]
+
+    def share(k, token):
+        part, token = spans[k].partial(beside_weights, field, other, True, token, spectra)
+        return lax.ppermute(part, "chan", beside), token
+
     output, grads, seconds, grad_others = None, [], [], []
-    for k in range(CHUNKS):
-        output, grad = local.forward(
-            own_weights, tables, bias, field, others[k], shares[k], spectra, cotangent, k, output
+    tables = (*synthesis_tables, *analysis_tables)
+    now, token = share(0, token)
+    for k in range(chunks):
+        later = None
+        if k + 1 < chunks:
+            later, token = share(k + 1, token)
+        output, grad, second, token = spans[k].forward(
+            own_weights, tables, bias, field, other, now, spectra, cotangent, token, output,
+            token,
         )
+        now = later
         grads.append(grad)
         grad_others.append(lax.ppermute(grad, "chan", across))
-        seconds.append(analyse_xy(grad, table_x, table_y))
-    grad_coeffs = analyse_zt(jnp.concatenate(seconds, axis=1), table_zt)
-    all_grad = lax.all_gather(grad_coeffs, "chan", axis=0, tiled=True)
+        seconds.append(second)
+    second = jnp.concatenate(seconds, axis=0)
+    grad_coeffs = analyse_zt(second, table_zt, count)
+    all_grad = gate(lax.all_gather(grad_coeffs, "chan", axis=0, tiled=True), grad_others[min(1, chunks - 1)])
     grad_weight = (coeffs.astype(jnp.float32)[:, None] * all_grad.astype(jnp.float32)[None]).astype(
         jnp.bfloat16
     )
@@ -314,22 +390,22 @@
         "cokm,okm->ckm", spec_weight, all_grad, preferred_element_type=jnp.float32
     ).astype(jnp.bfloat16)
     back = synthesise_zt(back_coeffs, table_zt)
-    grad_shares = [
-        lax.ppermute(
-            local_partial(local, beside_back, grads[k], grad_others[k]), "chan", beside
+
+    def share_back(k, token):
+        part, token = spans[k].partial(beside_back, grads[k], grad_others[k], False, token, back)
+        return lax.ppermute(part, "chan", beside), token
+
+    grad_field = None
+    now, token = share_back(0, token)
+    for k in range(chunks):
+        later = None
+        if k + 1 < chunks:
+            later, token = share_back(k + 1, token)
+        grad_field, token = spans[k].backward(
+            own_back, synthesis_tables, grads[k], grad_others[k], now, back, token, grad_field
         )
-        for k in range(CHUNKS)
-    ]
-    grad_field = None
-    for k in range(CHUNKS):
-        grad_field = local.backward(
-            own_back, tables, grads[k], grad_others[k], grad_shares[k], back, k, grad_field
-        )
+        now = later
     return (output.reshape(full_shape), grad_field.reshape(full_shape), grad_weight)
-
-
-def local_partial(local, weights, own, other):
-    return local.partial(weights, own, other, 0)
 
 
 def solution(mesh):

time: 742 us -> 618 us (0.83)
  waiting for transfers between devices: 427 us -> 362 us
  local copies, waits for them, and re-layouts: 72.5 us -> 37.1 us
  blocking collectives: 0 us -> 30.8 us
  matrix products: 31.3 us -> 3.34 us
  Pallas kernels: 135 us -> 126 us
    ppermute x4 -> x3, waiting for transfers between devices: 183 us -> 99.5 us  [body(): grad_others.append(lax.ppermute(grad, 'chan', across))]
    ppermute x12 -> x7, waiting for transfers between devices: 186 us -> 139 us  [the longest x1 110 us: body(): other = lax.ppermute(field, 'chan', across)]
    reduce_scatter x1, waiting for transfers between devices: 0.02 us -> 32 us  [body(): lax.psum_scatter(partial_value.astype(jnp.bfloat16), 'chan', scatter_dime...]
    all_to_all x0 -> x1, blocking collectives: none -> 30.8 us  [analyse_zt(): lax.all_to_all(second, 'slab', split_axis=1, concat_axis=0, tiled=True)]
    dot_general x10 -> x4, matrix products: 31.3 us -> 3.34 us  [the longest x2 1.75 us: analyse_zt(): jnp.einsum('mz,zjck->cjkm', table_zt, owned, preferred_element_type=jnp.f...]
    all_gather x1, waiting for transfers between devices: 0.01 us -> 23.1 us  [body(): lax.all_gather(grad_coeffs, 'chan', axis=0, tiled=True)]
    pallas_call x8 -> x6, Pallas kernels: 55.4 us -> 36.4 us  [partial(): pl.pallas_call(partial_kernel, grid=(self.steps,), in_specs=[self.whole(w...]
    all_to_all x4 -> x3, waiting for transfers between devices: 58.3 us -> 68.1 us  [the longest x2 47.5 us: synthesise_zt(): lax.all_to_all(slabs, 'slab', split_axis=0, concat_axis=1, tiled=True)]
  transfers between devices with their start and end apart: 22 -> 15, of which waited for: 11 -> 12; matrix products, arithmetic and copies ran while one was open for 10% -> 8% of each run, Pallas kernels for 16% -> 9%
where the time goes in v2:
time: 618 us; the launch traced here: 616 us
  waiting for transfers between devices  362 us (59%)
  Pallas kernels  126 us (20%)
  local copies, waits for them, and re-layouts  37.1 us (6%)
  blocking collectives  30.8 us (5%)
  starting transfers between devices  22.7 us (4%)
  other arithmetic  20.1 us (3%)
  between operations  14.3 us (2%)
    ppermute x1, waiting for transfers between devices, body(): other = lax.ppermute(field, 'chan', across)  110 us
    ppermute x3, waiting for transfers between devices, body(): grad_others.append(lax.ppermute(grad, 'chan', across))  99.5 us
    pallas_call x3, Pallas kernels, forward(): pl.pallas_call(forward_kernel, grid=(self.steps,), in_specs=specs, out_sp...  52.6 us
    all_to_all x2, waiting for transfers between devices, synthesise_zt(): lax.all_to_all(slabs, 'slab', split_axis=0, concat_axis=1, tiled=True)  47.5 us
    pallas_call x6, Pallas kernels, partial(): pl.pallas_call(partial_kernel, grid=(self.steps,), in_specs=[self.whole(w...  36.4 us
    reduce_scatter x1, waiting for transfers between devices, body(): lax.psum_scatter(partial_value.astype(jnp.bfloat16), 'chan', scatter_dime...  32 us
    all_to_all x1, blocking collectives, analyse_zt(): lax.all_to_all(second, 'slab', split_axis=1, concat_axis=0, tiled=True)  30.8 us
    pallas_call x3, Pallas kernels, backward(): pl.pallas_call(backward_kernel, grid=(self.steps,), in_specs=specs, out_s...  27.6 us
  transfers between devices with their start and end apart: 15, of which 12 were waited for; matrix products, arithmetic and copies ran while one was open for 8% of the time, Pallas kernels for 9%

profile of v2, /device:TPU:0, one launch (start us, length us, event | category | flops | bytes accessed | tf_op | source)
XLA Modules:
  0.0 616.2 jit_solution(5931506056027170173)
XLA Ops:
  14.7 9.3 %shard_map.76 = bf16[64,32,160]{2,1,0:T(8,128)(2,1)S(1)} custom-call(bf16[32,128]{1,0:T(8,128)(2,1)S(1)} %multiply_convert_fusion.3.ax_ref.refs_3_, bf16[640,160]{1,0:T(8,128)(2,1)S(1)} %bitcast.108, bf16[5,64,128,128]{3,2,1,0:T(8,128)(2,1)S(1)} %bitcast.86), custom_call_target="tpu_custom_call" | custom-call | flops 1 | bytes 1 | tf_op jit(solution)/shard_map/pallas_call | solution.py:232
  25.5 4.9 all-to-all-start
  35.3 20.6 %all-to-all-done = bf16[64,32,160]{2,0,1:T(8,128)(2,1)} async-done(((bf16[64,32,160]{2,0,1:T(8,128)(2,1)}), bf16[64,32,160]{2,0,1:T(8,128)(2,1)}, u32[]{:S(2)}, u32[]{:S(2)}) %all-to-all-start) | async-done | bytes 655392 | tf_op jit(solution)/shard_map/all_to_all | solution.py:48
  61.1 5.7 multiply_reduce_fusion.1
  66.8 32.0 %reduce-scatter.2.cloned.1.call-done = bf16[5,256,128]{2,1,0:T(8,128)(2,1)} async-done(((bf16[20,256,128]{2,1,0:T(8,128)(2,1)}), bf16[5,256,128]{2,1,0:T(8,128)(2,1)}) %reduce-scatter.2.cloned.1.call-update) | async-done | bytes 327696 | tf_op jit(solution)/shard_map/reduce_scatter | solution.py:359
  108.1 24.3 %all-to-all-done.1 = bf16[256,8,160]{2,1,0:T(8,128)(2,1)S(1)} async-done(((bf16[256,8,160]{2,1,0:T(8,128)(2,1)}), bf16[256,8,160]{2,1,0:T(8,128)(2,1)S(1)}, u32[]{:S(2)}, u32[]{:S(2)}) %all-to-all-start.1) | async-done | bytes 655392 | tf_op jit(solution)/shard_map/all_to_all | solution.py:66
  132.5 110.4 %collective-permute-done.other_ref.refs_7_ = bf16[5,64,128,128]{3,2,1,0:T(8,128)(2,1)} collective-permute-done((bf16[5,64,128,128]{3,2,1,0:T(8,128)(2,1)}, bf16[5,64,128,128]{3,2,1,0:T(8,128)(2,1)}, u32[]{:S(2)}, u32[]{:S(2)}) %collective-permute-start) | collective-permute-done | bytes 10485792 | tf_op jit(solution)/shard_map/ppermute | solution.py:353
  251.5 11.5 %shard_map.78 = (bf16[5,40,128,128]{3,2,1,0:T(8,128)(2,1)}, f32[8,128]{1,0:T(8,128)S(1)}) custom-call(bf16[80,160]{1,0:T(8,128)(2,1)S(1)} %mul.573.weight_ref, bf16[5,64,128,128]{3,2,1,0:T(8,128)(2,1)} %bitcast.82, bf16[5,64,128,128]{3,2,1,0:T(8,128)(2,1)} %collective-permute-done.other_ref.refs_7_, f32[8,128]{1,0:T(8,128)S(1)} %get-tuple-element.33.token_ref, ...), custom_call_target="tpu_custom_call" | custom-call | flops 1 | bytes 1 | tf_op jit(solution)/shard_map/pallas_call | solution.py:243
  264.0 13.6 %collective-permute-done.1.refs_8_ = bf16[5,16,128,128]{3,2,1,0:T(8,128)(2,1)} collective-permute-done((bf16[5,16,128,128]{3,2,1,0:T(8,128)(2,1)}, bf16[5,16,128,128]{3,2,1,0:T(8,128)(2,1)}, u32[]{:S(2)}, u32[]{:S(2)}) %collective-permute-start.1) | collective-permute-done | bytes 2621472 | tf_op jit(solution)/shard_map/ppermute | solution.py:366
  277.6 13.9 %shard_map.79 = (bf16[5,64,128,128]{3,2,1,0:T(8,128)(2,1)}, bf16[5,16,128,128]{3,2,1,0:T(8,128)(2,1)}, bf16[16,32,160]{2,1,0:T(8,128)(2,1)S(1)}, f32[8,128]{1,0:T(8,128)S(1)}) custom-call(bf16[80,160]{1,0:T(8,128)(2,1)S(1)} %mul.555.refs_0_, bf16[128,32]{1,0:T(8,128)(2,1)S(1)} %multiply_convert_fusion.2.refs_1_, bf16[160,640]{1,0:T(8,128)(2,1)S(1)} %bitcast.102, ...), custom_call_target="tpu_custom_call" | custom-call | flops 1 | bytes 1 | tf_op jit(solution)/shard_map/pallas_call | solution.py:272
  297.4 30.7 %shard_map.81 = (bf16[5,64,128,128]{3,2,1,0:T(8,128)(2,1)}, bf16[5,40,128,128]{3,2,1,0:T(8,128)(2,1)}, bf16[40,32,160]{2,1,0:T(8,128)(2,1)S(1)}, f32[8,128]{1,0:T(8,128)S(1)}) custom-call(bf16[80,160]{1,0:T(8,128)(2,1)S(1)} %mul.555.refs_0_, bf16[128,32]{1,0:T(8,128)(2,1)S(1)} %multiply_convert_fusion.2.refs_1_, ...), custom_call_target="tpu_custom_call", output_to_operand_aliasing={{0}: (13, {})} | custom-call | flops 1 | bytes 1 | tf_op jit(solution)/shard_map/pallas_call | solution.py:272
  332.9 8.0 %shard_map.82 = (bf16[5,64,128,128]{3,2,1,0:T(8,128)(2,1)}, bf16[5,8,128,128]{3,2,1,0:T(8,128)(2,1)S(1)}, bf16[8,32,160]{2,1,0:T(8,128)(2,1)S(1)}, f32[8,128]{1,0:T(8,128)S(1)}) custom-call(bf16[80,160]{1,0:T(8,128)(2,1)S(1)} %mul.555.refs_0_, bf16[128,32]{1,0:T(8,128)(2,1)S(1)} %multiply_convert_fusion.2.refs_1_, ...), custom_call_target="tpu_custom_call", output_to_operand_aliasing={{0}: (13, {})} | custom-call | flops 1 | bytes 1 | tf_op jit(solution)/shard_map/pallas_call | solution.py:272
  341.6 30.8 %all_to_all.66 = bf16[64,32,160]{2,0,1:T(8,128)(2,1)} all-to-all(bf16[64,32,160]{2,0,1:T(8,128)(2,1)S(1)} %copy.57), channel_id=1, replica_groups=mesh['groups'=2,'slab'=4,'chan'=4] {'slab'}, dimensions={1} | all-to-all | bytes 1310720 | tf_op jit(solution)/shard_map/all_to_all | solution.py:48
  379.9 23.1 %all-gather.2.cloned.1.call-done.value_ref = bf16[20,256,128]{2,1,0:T(8,128)(2,1)} async-done(((bf16[5,256,128]{2,1,0:T(8,128)(2,1)}), bf16[20,256,128]{2,1,0:T(8,128)(2,1)}) %all-gather.2.cloned.1.call-update) | async-done | bytes 1310736 | tf_op jit(solution)/shard_map/all_gather | solution.py:385
  403.0 76.4 %collective-permute-done.6.refs_0_.other_ref.refs_4_ = bf16[5,40,128,128]{3,2,1,0:T(8,128)(2,1)} collective-permute-done((bf16[5,40,128,128]{3,2,1,0:T(8,128)(2,1)}, bf16[5,40,128,128]{3,2,1,0:T(8,128)(2,1)}, u32[]{:S(2)}, u32[]{:S(2)}) %collective-permute-start.6) | collective-permute-done | bytes 6553632 | tf_op jit(solution)/shard_map/ppermute | solution.py:381
  489.0 5.1 all-to-all-start.3
  495.3 23.2 %all-to-all-done.3 = bf16[256,8,160]{2,1,0:T(8,128)(2,1)S(1)} async-done(((bf16[256,8,160]{2,1,0:T(8,128)(2,1)}), bf16[256,8,160]{2,1,0:T(8,128)(2,1)S(1)}, u32[]{:S(2)}, u32[]{:S(2)}) %all-to-all-start.3) | async-done | bytes 655392 | tf_op jit(solution)/shard_map/all_to_all | solution.py:66
  520.8 14.0 %collective-permute-done.5.other_ref.refs_4_ = bf16[5,16,128,128]{3,2,1,0:T(8,128)(2,1)} collective-permute-done((bf16[5,16,128,128]{3,2,1,0:T(8,128)(2,1)}, bf16[5,16,128,128]{3,2,1,0:T(8,128)(2,1)}, u32[]{:S(2)}, u32[]{:S(2)}) %collective-permute-start.5) | collective-permute-done | bytes 2621472 | tf_op jit(solution)/shard_map/ppermute | solution.py:381
  534.8 5.0 shard_map.84
  539.8 11.5 %shard_map.85 = (bf16[5,40,128,128]{3,2,1,0:T(8,128)(2,1)}, f32[8,128]{1,0:T(8,128)S(1)}) custom-call(bf16[80,160]{1,0:T(8,128)(2,1)S(1)} %mul.594.weight_ref, bf16[5,40,128,128]{3,2,1,0:T(8,128)(2,1)} %get-tuple-element.49.own_ref.refs_3_, bf16[5,40,128,128]{3,2,1,0:T(8,128)(2,1)} %collective-permute-done.6.refs_0_.other_ref.refs_4_, ...), custom_call_target="tpu_custom_call" | custom-call | flops 1 | bytes 1 | tf_op jit(solution)/shard_map/pallas_call | solution.py:243
  553.8 12.2 %collective-permute-done.7.refs_5_ = bf16[5,16,128,128]{3,2,1,0:T(8,128)(2,1)} collective-permute-done((bf16[5,16,128,128]{3,2,1,0:T(8,128)(2,1)}, bf16[5,16,128,128]{3,2,1,0:T(8,128)(2,1)}, u32[]{:S(2)}, u32[]{:S(2)}) %collective-permute-start.7) | collective-permute-done | bytes 2621472 | tf_op jit(solution)/shard_map/ppermute | solution.py:396
  566.0 7.5 %shard_map.86 = (bf16[5,64,128,128]{3,2,1,0:T(8,128)(2,1)}, f32[8,128]{1,0:T(8,128)S(1)}) custom-call(bf16[80,160]{1,0:T(8,128)(2,1)S(1)} %mul.591.refs_0_, bf16[128,32]{1,0:T(8,128)(2,1)S(1)} %multiply_convert_fusion.2.refs_1_, bf16[160,640]{1,0:T(8,128)(2,1)S(1)} %bitcast.105, bf16[5,16,128,128]{3,2,1,0:T(8,128)(2,1)} %get-tuple-element.44.own_ref.refs_3_, ...), custom_call_target="tpu_custom_call" | custom-call | flops 1 | bytes 1 | tf_op jit(solution)/shard_map/pallas_call | solution.py:298
  573.5 9.2 %collective-permute-done.4.other_ref.refs_4_ = bf16[5,8,128,128]{3,2,1,0:T(8,128)(2,1)} collective-permute-done((bf16[5,8,128,128]{3,2,1,0:T(8,128)(2,1)S(1)}, bf16[5,8,128,128]{3,2,1,0:T(8,128)(2,1)}, u32[]{:S(2)}, u32[]{:S(2)}) %collective-permute-start.4) | collective-permute-done | bytes 1310752 | tf_op jit(solution)/shard_map/ppermute | solution.py:381
  589.3 16.0 %shard_map.88 = (bf16[5,64,128,128]{3,2,1,0:T(8,128)(2,1)}, f32[8,128]{1,0:T(8,128)S(1)}) custom-call(bf16[80,160]{1,0:T(8,128)(2,1)S(1)} %mul.591.refs_0_, bf16[128,32]{1,0:T(8,128)(2,1)S(1)} %multiply_convert_fusion.2.refs_1_, bf16[160,640]{1,0:T(8,128)(2,1)S(1)} %bitcast.106, ...), custom_call_target="tpu_custom_call", output_to_operand_aliasing={{0}: (8, {})} | custom-call | flops 1 | bytes 1 | tf_op jit(solution)/shard_map/pallas_call | solution.py:298
  (95 shorter events, 83.2 us)
Async XLA Ops:
  7.2 235.7 %collective-permute-start = (bf16[5,64,128,128]{3,2,1,0:T(8,128)(2,1)}, bf16[5,64,128,128]{3,2,1,0:T(8,128)(2,1)}, u32[]{:S(2)}, u32[]{:S(2)}) collective-permute-start(bf16[5,64,128,128]{3,2,1,0:T(8,128)(2,1)} %bitcast.81), channel_id=1, source_target_pairs={{0,2},{1,3},{2,0},{3,1},{4,6},{5,7},{6,4},{7,5},{8,10},{9,11},{10,... | collective-permute-start | bytes 31457288 | tf_op jit(solution)/shard_map/ppermute | solution.py:353
  10.7 4.0 copy-start
  25.5 30.4 %all-to-all-start = ((bf16[64,32,160]{2,0,1:T(8,128)(2,1)}), bf16[64,32,160]{2,0,1:T(8,128)(2,1)}, u32[]{:S(2)}, u32[]{:S(2)}) async-start(bf16[64,32,160]{2,0,1:T(8,128)(2,1)} %copy.49), calls=%async_computation | async-start | bytes 2097152 | tf_op jit(solution)/shard_map/all_to_all | solution.py:48
  30.4 68.4 %reduce-scatter.2.cloned.1.call-start = ((), (), s32[]{:S(2)}) async-start(), calls=%async_computation.5 | async-start | bytes 1638400 | tf_op jit(solution)/shard_map/reduce_scatter | solution.py:359
  66.7 39.7 %copy-start.10 = (bf16[20,20]{1,0:T(8,128)(2,1)S(1)}, bf16[20,20]{1,0:T(8,128)(2,1)}, u32[]{:S(2)}) copy-start(bf16[20,20]{1,0:T(8,128)(2,1)} %param.7) | copy-start | bytes 2404
  101.8 30.6 %all-to-all-start.1 = ((bf16[256,8,160]{2,1,0:T(8,128)(2,1)}), bf16[256,8,160]{2,1,0:T(8,128)(2,1)S(1)}, u32[]{:S(2)}, u32[]{:S(2)}) async-start(bf16[256,8,160]{2,1,0:T(8,128)(2,1)} %copy.53), calls=%async_computation.2 | async-start | bytes 2097152 | tf_op jit(solution)/shard_map/all_to_all | solution.py:66
  106.4 296.6 %all-gather.2.cloned.1.call-start = ((), (), s32[]{:S(2)}) async-start(), calls=%async_computation.6 | async-start | bytes 1638400 | tf_op jit(solution)/shard_map/all_gather | solution.py:385
  242.9 4.0 copy-start.1
  251.5 12.0 %copy-start.9 = (bf16[5,16,10,16]{3,2,1,0:T(8,128)(2,1)S(1)}, bf16[5,16,10,16]{3,2,1,0:T(8,128)(2,1)}, u32[]{:S(2)}) copy-start(bf16[5,16,10,16]{3,2,1,0:T(8,128)(2,1)} %get-tuple-element.75) | copy-start | bytes 76804
  251.5 26.1 %copy-start.4 = (f32[5]{0:T(128)S(1)}, f32[5]{0:T(128)}, u32[]{:S(2)}) copy-start(f32[5]{0:T(128)} %refs_5_.5) | copy-start | bytes 64
  263.0 34.4 %collective-permute-start.3 = (bf16[5,40,128,128]{3,2,1,0:T(8,128)(2,1)}, bf16[5,40,128,128]{3,2,1,0:T(8,128)(2,1)}, u32[]{:S(2)}, u32[]{:S(2)}) collective-permute-start(bf16[5,40,128,128]{3,2,1,0:T(8,128)(2,1)} %get-tuple-element.37), channel_id=1, source_target_pairs={{0,1},{1,0},{2,3},{3,2},{4,5},{5,4},{6,7},{7,6},{8,9},{9,8},{10,11... | collective-permute-start | bytes 19660808 | tf_op jit(solution)/shard_map/ppermute | solution.py:366
  263.0 14.6 %collective-permute-start.1 = (bf16[5,16,128,128]{3,2,1,0:T(8,128)(2,1)}, bf16[5,16,128,128]{3,2,1,0:T(8,128)(2,1)}, u32[]{:S(2)}, u32[]{:S(2)}) collective-permute-start(bf16[5,16,128,128]{3,2,1,0:T(8,128)(2,1)} %get-tuple-element.32), channel_id=1, source_target_pairs={{0,1},{1,0},{2,3},{3,2},{4,5},{5,4},{6,7},{7,6},{8,9},{9,8},{10,11... | collective-permute-start | bytes 7864328 | tf_op jit(solution)/shard_map/ppermute | solution.py:366
  291.5 4.0 copy-start.2
  328.1 151.3 %collective-permute-start.6 = (bf16[5,40,128,128]{3,2,1,0:T(8,128)(2,1)}, bf16[5,40,128,128]{3,2,1,0:T(8,128)(2,1)}, u32[]{:S(2)}, u32[]{:S(2)}) collective-permute-start(bf16[5,40,128,128]{3,2,1,0:T(8,128)(2,1)} %get-tuple-element.49.own_ref.refs_3_), channel_id=1, source_target_pairs={{0,2},{1,3},{2,0},{3,1},{4,6},{5,7},{6,4},{7,5},{8,10},{9,11},{10,... | collective-permute-start | bytes 19660808 | tf_op jit(solution)/shard_map/ppermute | solution.py:381
  329.8 3.0 collective-permute-start.2
  379.3 155.5 %collective-permute-start.5 = (bf16[5,16,128,128]{3,2,1,0:T(8,128)(2,1)}, bf16[5,16,128,128]{3,2,1,0:T(8,128)(2,1)}, u32[]{:S(2)}, u32[]{:S(2)}) collective-permute-start(bf16[5,16,128,128]{3,2,1,0:T(8,128)(2,1)} %get-tuple-element.44.own_ref.refs_3_), channel_id=1, source_target_pairs={{0,2},{1,3},{2,0},{3,1},{4,6},{5,7},{6,4},{7,5},{8,10},{9,11},{10,... | collective-permute-start | bytes 7864328 | tf_op jit(solution)/shard_map/ppermute | solution.py:381
  489.0 29.5 %all-to-all-start.3 = ((bf16[256,8,160]{2,1,0:T(8,128)(2,1)}), bf16[256,8,160]{2,1,0:T(8,128)(2,1)S(1)}, u32[]{:S(2)}, u32[]{:S(2)}) async-start(bf16[256,8,160]{2,1,0:T(8,128)(2,1)} %copy.61), calls=%async_computation.4 | async-start | bytes 2097152 | tf_op jit(solution)/shard_map/all_to_all | solution.py:66
  539.8 13.8 %copy-start.8 = (bf16[5,16,10,16]{3,2,1,0:T(8,128)(2,1)S(1)}, bf16[5,16,10,16]{3,2,1,0:T(8,128)(2,1)}, u32[]{:S(2)}) copy-start(bf16[5,16,10,16]{3,2,1,0:T(8,128)(2,1)} %get-tuple-element.74) | copy-start | bytes 76804
  551.4 37.9 %collective-permute-start.9 = (bf16[5,40,128,128]{3,2,1,0:T(8,128)(2,1)}, bf16[5,40,128,128]{3,2,1,0:T(8,128)(2,1)}, u32[]{:S(2)}, u32[]{:S(2)}) collective-permute-start(bf16[5,40,128,128]{3,2,1,0:T(8,128)(2,1)} %get-tuple-element.55), channel_id=1, source_target_pairs={{0,1},{1,0},{2,3},{3,2},{4,5},{5,4},{6,7},{7,6},{8,9},{9,8},{10,11... | collective-permute-start | bytes 19660808 | tf_op jit(solution)/shard_map/ppermute | solution.py:396
  551.4 14.6 %collective-permute-start.7 = (bf16[5,16,128,128]{3,2,1,0:T(8,128)(2,1)}, bf16[5,16,128,128]{3,2,1,0:T(8,128)(2,1)}, u32[]{:S(2)}, u32[]{:S(2)}) collective-permute-start(bf16[5,16,128,128]{3,2,1,0:T(8,128)(2,1)} %get-tuple-element.50), channel_id=1, source_target_pairs={{0,1},{1,0},{2,3},{3,2},{4,5},{5,4},{6,7},{7,6},{8,9},{9,8},{10,11... | collective-permute-start | bytes 7864328 | tf_op jit(solution)/shard_map/ppermute | solution.py:396
  551.9 30.8 %collective-permute-start.4 = (bf16[5,8,128,128]{3,2,1,0:T(8,128)(2,1)S(1)}, bf16[5,8,128,128]{3,2,1,0:T(8,128)(2,1)}, u32[]{:S(2)}, u32[]{:S(2)}) collective-permute-start(bf16[5,8,128,128]{3,2,1,0:T(8,128)(2,1)S(1)} %get-tuple-element.43.own_ref.refs_3_), channel_id=1, source_target_pairs={{0,2},{1,3},{2,0},{3,1},{4,6},{5,7},{6,4},{7,5},{8,10},{9,11},{10,... | collective-permute-start | bytes 3932168 | tf_op jit(solution)/shard_map/ppermute | solution.py:381
  566.0 18.7 %copy-start.5 = (f32[20,256,128]{2,1,0:T(8,128)S(1)}, f32[20,256,128]{2,1,0:T(8,128)}, u32[]{:S(2)}) copy-start(f32[20,256,128]{2,1,0:T(8,128)} %get-tuple-element.61) | copy-start | bytes 7864324
  566.0 18.7 %copy-start.7 = (f32[5,256,128]{2,1,0:T(8,128)S(1)}, f32[5,256,128]{2,1,0:T(8,128)}, u32[]{:S(2)}) copy-start(f32[5,256,128]{2,1,0:T(8,128)} %get-tuple-element.63) | copy-start | bytes 1966084
  584.6 20.8 %collective-permute-start.8 = (bf16[5,8,128,128]{3,2,1,0:T(8,128)(2,1)S(1)}, bf16[5,8,128,128]{3,2,1,0:T(8,128)(2,1)S(1)}, u32[]{:S(2)}, u32[]{:S(2)}) collective-permute-start(bf16[5,8,128,128]{3,2,1,0:T(8,128)(2,1)S(1)} %get-tuple-element.54), channel_id=1, source_target_pairs={{0,1},{1,0},{2,3},{3,2},{4,5},{5,4},{6,7},{7,6},{8,9},{9,8},{10,11... | collective-permute-start | bytes 3932168 | tf_op jit(solution)/shard_map/ppermute | solution.py:396
  (2 other events, 2.3 us)
Sparse Core Ops, SparseCore 0:
  66.9 31.8 reduce-scatter.1
  379.4 23.5 all-gather.1
